TPU v7x, 32 devices: a whole 2x2x4 slice. The times are simulated.
32 devices in a mesh: space: 16 (over z, y, x), batch: 2 (over core).
Axes of the slice: x: 2, y: 2, z: 4, core: 2. Of those that a mesh axis runs over, the one named last changes fastest.
Arguments:
- volume: bfloat16 [4, 2, 64, 128, 128], P(None, 'batch', 'space'), may hold values from -72 to 72
- kernel_one: bfloat16 [108, 32], replicated, may hold values from -0.625 to 0.625
- kernel_two: bfloat16 [864, 64], replicated, may hold values from -0.21875 to 0.21875
- cotangent: bfloat16 [64, 2, 16, 1024], P(None, 'batch', 'space'), may hold values from -6 to 6
Outputs:
- features: bfloat16 [64, 2, 16, 1024], P(None, 'batch', None, 'space')
- factor_in_one: float32 [108, 108], replicated
- factor_in_two: float32 [864, 864], replicated
- factor_out_one: float32 [32, 32], replicated
- factor_out_two: float32 [64, 64], replicated
- weight_grad_one: float32 [108, 32], replicated
- weight_grad_two: float32 [864, 64], replicated
All inputs are finite; a program needn't handle non-finite values.
Results may differ from a plain program's by a relative error of at most 0.007.
Values may be sent and summed in bfloat16 or wider, within the bound.
No kernel may reach another device: no remote copies, remote signals or barrier semaphores. Data moves between devices by JAX's collectives and lax.ppermute only.
A program may use at most 128 MiB of HBM per device.

v0:
```python
import functools
import math

import jax
import jax.numpy as jnp
import numpy as np
from jax import lax
from jax.experimental import pallas as pl
from jax.experimental.pallas import tpu as pltpu
from jax.sharding import PartitionSpec as P

F32 = jnp.float32
BF16 = jnp.bfloat16
LANES = 128
TAPS = 27
MIB = 1024 * 1024


def up_to(count, unit):
    return -(-count // unit) * unit


def split_columns(plane, quarter):
    table = np.zeros((4, plane, 5, 4, quarter), np.float32)
    for group in range(4):
        for q in range(5):
            for cell in range(quarter):
                x = 4 * cell + q - 1
                if 0 <= x < plane:
                    table[group, x, q, group, cell] = 1.0
    return table.reshape(4 * plane, 5 * 4 * quarter)


def patch_rows(channels, first, planes, hidden_planes, rows):
    width = up_to(25 * channels * planes, 16)
    table = np.zeros((len(hidden_planes), 2, 2, rows, width), np.float32)
    for at, j in enumerate(hidden_planes):
        for a in range(3):
            plane = 2 * j + a - first
            if not 0 <= plane < planes:
                continue
            for py, px, c, b, e in np.ndindex(2, 2, channels, 3, 3):
                source = (((2 * px + e) * channels + c) * planes + plane) * 5 + 2 * py + b
                table[at, py, px, c * TAPS + a * 9 + b * 3 + e, source] = 1.0
    return table.reshape(len(hidden_planes) * 4, rows, width)


def dot(first, second):
    return jnp.dot(first, second, preferred_element_type=F32)


def dot_nt(first, second):
    return lax.dot_general(first, second, (((1,), (1,)), ((), ())), preferred_element_type=F32)


def gelu_parts(value):
    square = value * value
    tangent = jnp.tanh(0.7978845608028654 * (value + 0.044715 * value * square))
    half = 0.5 * (1.0 + tangent)
    return value * half, half, tangent, square


def gelu_and_slope(value):
    act, half, tangent, square = gelu_parts(value)
    slope = half + 0.5 * value * (1.0 - tangent * tangent) * (
        0.7978845608028654 * (1.0 + 3.0 * 0.044715 * square)
    )
    return act, slope


def prepare_kernel(k1t_ref, k2t_ref, halo_rows_ref, own_rows_ref, halo_wide_ref, own_wide_ref, back_ref, k2_rows):
    hidden, rows_one = k1t_ref.shape
    rows_pad = halo_rows_ref.shape[1]
    k1t = jnp.pad(k1t_ref[...].astype(F32), ((0, 0), (0, rows_pad - rows_one))).astype(BF16)
    for rows_ref, wide_ref in ((halo_rows_ref, halo_wide_ref), (own_rows_ref, own_wide_ref)):
        for block in range(rows_ref.shape[0]):
            wide_ref[block * hidden : (block + 1) * hidden, :] = dot(k1t, rows_ref[block]).astype(BF16)
    out_chan, rows_two = k2t_ref.shape
    for at in range(0, rows_two, LANES):
        tall = min(LANES, rows_two - at)
        block = k2t_ref[:, at : at + tall].astype(F32)
        if tall < LANES:
            block = jnp.pad(block, ((0, 0), (0, LANES - tall)))
        k2_rows[at : at + tall, :out_chan] = block.T[:tall, :]
    taps = [k2_rows[pl.ds(tap, hidden, stride=TAPS), :][:, :out_chan] for tap in range(TAPS)]
    nothing = jnp.zeros_like(taps[0])

    def tap_for(parity, shift):
        if parity == 0:
            return 1 if shift == 0 else None
        return 2 if shift == 0 else 0

    for j in (1, 2):
        for py in range(2):
            for px in range(2):
                blocks = []
                for above in range(2):
                    a = {(1, 0): 1, (2, 0): 2, (2, 1): 0}.get((j, above))
                    for sy in range(2):
                        for sx in range(2):
                            b, e = tap_for(py, sy), tap_for(px, sx)
                            there = a is not None and b is not None and e is not None
                            blocks.append(taps[a * 9 + b * 3 + e] if there else nothing)
                start = ((j - 1) * 4 + py * 2 + px) * hidden
                back_ref[start : start + hidden, :] = jnp.concatenate(blocks, axis=1).astype(BF16)


def split_cells(planes, split_ref, cells_ref, rows_scr, lhs_scr, cells_scr):
    plane = planes[0].shape[0]
    pitch = plane + 8
    for at, source in enumerate(planes):
        start = at * pitch
        rows_scr[start : start + 8, :] = jnp.zeros((8, plane), F32)
        rows_scr[start + 8 : start + pitch, :] = source[...].astype(F32)
    for pair in range(len(planes) // 2):
        pieces = []
        for member in range(2):
            start = (pair * 2 + member) * pitch + 8
            tiles = [rows_scr[pl.ds(start + t, 8, stride=16), :] for t in range(-1, 16)]
            for q in range(5):
                pieces.append(jnp.concatenate([tiles[4 * group + q] for group in range(4)], axis=1))
        lhs_scr[pair * 80 : (pair + 1) * 80, :] = jnp.concatenate(pieces, axis=0).astype(BF16)
    total_rows = len(planes) * 40
    chunk = 160
    for part in range(total_rows // chunk):
        product = dot(lhs_scr[part * chunk : (part + 1) * chunk, :], split_ref[...])
        for q in range(5):
            start = q * total_rows + part * chunk
            cells_scr[start : start + chunk, :] = product[:, q * LANES : (q + 1) * LANES]
    filled = 5 * total_rows
    width = cells_ref.shape[0]
    if filled < 8 * width:
        cells_scr[filled : 8 * width, :] = jnp.zeros((8 * width - filled, LANES), F32)
    for yh in range(8):
        cells_ref[:, yh * LANES : (yh + 1) * LANES] = cells_scr[pl.ds(yh, width, stride=8), :].astype(BF16)


def own_kernel(
    vol_ref, wide_ref, split_ref, rows_ref,
    part_ref, act_ref, slope_ref, p1_ref, in_one_ref, rows_scr, lhs_scr, cells_scr, cells_ref,
):
    channels, own = vol_ref.shape[0], vol_ref.shape[1]
    planes = [vol_ref.at[c, z] for c in range(channels) for z in range(own)]
    split_cells(planes, split_ref, cells_ref, rows_scr, lhs_scr, cells_scr)
    pre = dot(wide_ref[...], cells_ref[...])
    tall = part_ref.shape[0]
    part_ref[...] = pre[:tall, :]
    quarter = tall // 4
    for at in range(0, tall, quarter):
        act, slope = gelu_and_slope(pre[tall + at : tall + at + quarter, :])
        act_ref[at : at + quarter, :] = act
        slope_ref[at : at + quarter, :] = slope
    blocks, rows_pad, width = rows_ref.shape
    p1 = dot(rows_ref[...].reshape(blocks * rows_pad, width), cells_ref[...]).astype(BF16)
    total = jnp.zeros((rows_pad, rows_pad), F32)
    for block in range(blocks):
        piece = p1[block * rows_pad : (block + 1) * rows_pad, :]
        p1_ref[block] = piece
        if block >= blocks // 2:
            total += dot_nt(piece, piece)
    in_one_ref[...] = total


def forward_kernel(
    scale, halo_ref, wide_ref, split_ref, part_ref, act_ref, k2t_ref, cot_ref,
    grad_ref, p2_ref, slope_ref, cells_ref, *rest,
):
    feat_refs, (rows_scr, lhs_scr, cells_scr, p2_scr, feat_scr) = rest[:-5], rest[-5:]
    channels, halo = halo_ref.shape[0], halo_ref.shape[1]
    planes = [halo_ref.at[c, z] for c in range(channels) for z in range(halo)]
    split_cells(planes, split_ref, cells_ref, rows_scr, lhs_scr, cells_scr)
    cells = cells_ref.shape[1]
    lane = lax.broadcasted_iota(jnp.int32, (1, cells), 1)
    side = math.isqrt(cells)
    not_left = (lane % side) != 0
    not_top = lane >= side
    tall = part_ref.shape[0]
    hidden = tall // 4
    rows_two = hidden * TAPS
    for j in (2, 1, 0):
        if j < 2:
            pre = dot(wide_ref[j * tall : (j + 1) * tall, :], cells_ref[...])
            if j == 1:
                pre = pre + part_ref[...]
        for parity in range(4):
            rows = slice(parity * hidden, (parity + 1) * hidden)
            if j == 2:
                act = act_ref[rows, :]
            elif j == 1:
                act, slope = gelu_and_slope(pre[rows, :])
                slope_ref[rows, :] = slope
            else:
                act = gelu_parts(pre[rows, :])[0]
            py, px = parity // 2, parity % 2
            for b in ((1,) if py == 0 else (2, 0)):
                for e in ((1,) if px == 0 else (2, 0)):
                    moved = act
                    distance = (side if b == 0 else 0) + (1 if e == 0 else 0)
                    if distance:
                        moved = pltpu.roll(act, distance, axis=1)
                    if b == 0:
                        moved = jnp.where(not_top, moved, 0.0)
                    if e == 0:
                        moved = jnp.where(not_left, moved, 0.0)
                    for k in range(cells // LANES):
                        start = k * rows_two + j * 9 + b * 3 + e
                        p2_scr[pl.ds(start, hidden, stride=TAPS), :] = moved[:, k * LANES : (k + 1) * LANES]
    for k in range(cells // LANES):
        p2_ref[:rows_two, k * LANES : (k + 1) * LANES] = p2_scr[k * rows_two : (k + 1) * rows_two, :].astype(BF16)
    p2_ref[rows_two:, :] = jnp.zeros((p2_ref.shape[0] - rows_two, cells), BF16)
    act, slope = gelu_and_slope(dot(k2t_ref[...], p2_ref[:rows_two, :]))
    grad_ref[...] = (cot_ref[...].astype(F32) * scale * slope).astype(BF16)
    owned = cells // feat_scr.shape[0]
    rows = act.shape[0] * owned // LANES
    count = LANES // owned
    place = lax.broadcasted_iota(jnp.int32, (1, LANES), 1) // owned
    for k in range(cells // LANES):
        tile = act[:, k * LANES : (k + 1) * LANES]
        for u in range(count):
            total = jnp.zeros((rows, LANES), F32)
            for m in range(count):
                block = tile[m * rows : (m + 1) * rows, :]
                if m != u:
                    block = pltpu.roll(block, ((m - u) * owned) % LANES, axis=1)
                total = jnp.where(place == m, block, total)
            if rows < feat_scr.shape[1]:
                total = jnp.pad(total, ((0, feat_scr.shape[1] - rows), (0, 0)))
            feat_scr[k * count + u] = total.astype(BF16)
    owners = feat_refs[0].shape[0]
    cube = lax.axis_index("space") // owners
    for change, feat_ref in enumerate(feat_refs):
        feat_ref[...] = feat_scr[pl.ds((cube ^ change) * owners, owners)]


def large_places(rows_two, out_chan):
    panels = -(-rows_two // LANES)
    pairs = (panels + 1) // 2
    middle = pairs // 2 * 2
    names = [("block", i, j) for j in range(middle, panels) for i in range(middle)]
    names += [("block", i, j) for j in range(middle) for i in range(j)]
    names += [("block", i, j) for j in range(middle, panels) for i in range(middle, j)]
    names += [("pair", p) for p in range(pairs)]
    cross = middle * (panels - middle)
    weights = [("weight_two", j) for j in range(panels - 1)]
    half = (len(names) * LANES + len(weights) * out_chan) // 2
    early = (half - cross * LANES) // out_chan
    order = [(name, LANES) for name in names[:cross]] + [(name, out_chan) for name in weights[:early]]
    order += [(name, LANES) for name in names[cross:]] + [(name, out_chan) for name in weights[early:]]
    places, at = {}, 0
    for name, rows in order:
        places[name] = at
        at += rows
    return panels, middle, places, at


def square_iotas():
    return (
        lax.broadcasted_iota(jnp.int32, (LANES, LANES), 0),
        lax.broadcasted_iota(jnp.int32, (LANES, LANES), 1),
    )


def diagonal_row(block):
    row, col = square_iotas()
    return jnp.sum(jnp.where(row == col, block, 0.0), axis=0, keepdims=True)


def two_in_one(upper, lower):
    row, col = square_iotas()
    return jnp.where(row <= col, upper, lower)


def first_of(block, turned):
    row, col = square_iotas()
    return jnp.where(row <= col, block, turned)


def second_of(block, turned, diagonal):
    row, col = square_iotas()
    return jnp.where(row > col, block, jnp.where(row == col, diagonal, turned))


def square(block):
    return jnp.pad(block, ((0, LANES - block.shape[0]), (0, LANES - block.shape[1])))


def padded_lanes(block):
    return jnp.pad(block, ((0, 0), (0, LANES - block.shape[1])))


def put(packed, at, block):
    half = packed.shape[1]
    done = 0
    while done < block.shape[0]:
        side, row = divmod(at + done, half)
        count = min(block.shape[0] - done, half - row)
        packed[side, row : row + count, :] = block[done : done + count, :].astype(BF16)
        done += count


def sums_kernel(
    places, rows_two, p2_ref, grad_ref, mine_ref, other_ref, done_ref, packed, product_scr, sems,
):
    done_ref[...] = jnp.zeros_like(done_ref)
    panels = p2_ref.shape[0] // LANES
    used = rows_two - (panels - 1) * LANES
    lane = lax.broadcasted_iota(jnp.int32, (1, LANES), 1)
    weight_two = dot_nt(grad_ref[...], p2_ref[...])
    out_chan = weight_two.shape[0]
    last = weight_two[:, (panels - 1) * LANES :]
    spare = LANES - used
    diagonals = []
    for j in range(0, panels, 2):
        wide = min(2, panels - j)
        tall = (j + wide) * LANES
        product = product_scr.at[(j // 2) % 2]
        product[:tall, : wide * LANES] = dot_nt(p2_ref[:tall, :], p2_ref[j * LANES : tall, :])
        for k in range(wide):
            columns = slice(k * LANES, (k + 1) * LANES)
            for i in range(j + k):
                block = product[i * LANES : (i + 1) * LANES, columns]
                if j + k == panels - 1 and i * spare < used:
                    piece = pltpu.roll(last, used - i * spare, axis=1)
                    top = jnp.where(lane >= used, piece, block[:out_chan, :])
                    block = jnp.concatenate([top, block[out_chan:, :]], axis=0)
                put(packed, places["block", i, j + k], block)
        first = product[j * LANES : (j + 1) * LANES, :LANES]
        if wide == 2:
            second = product[(j + 1) * LANES : tall, LANES:]
        else:
            second = square(dot_nt(grad_ref[...], grad_ref[...]))
        diagonals.append(diagonal_row(second))
        block = two_in_one(first, second)
        if wide == 1:
            row, _ = square_iotas()
            for at, diagonal in enumerate(diagonals):
                block = jnp.where(row == used + at, diagonal, block)
        put(packed, places["pair", j // 2], block)
    for j in range(panels - 1):
        put(packed, places["weight_two", j], weight_two[:, j * LANES : (j + 1) * LANES])
    core = lax.axis_index("batch")
    mine = pltpu.make_async_copy(packed.at[core], mine_ref, sems.at[0])
    other = pltpu.make_async_copy(packed.at[1 - core], other_ref, sems.at[1])
    other.start()
    mine.start()
    other.wait()
    mine.wait()


def shifted_up(source, scr):
    out_chan, cells = source.shape
    side = math.isqrt(cells)
    lane = lax.broadcasted_iota(jnp.int32, (1, cells), 1)
    value = source[...].astype(F32)
    for sy in range(2):
        for sx in range(2):
            moved = value
            distance = sy * side + sx
            if distance:
                moved = pltpu.roll(value, cells - distance, axis=1)
            if sy:
                moved = jnp.where(lane < cells - side, moved, 0.0)
            if sx:
                moved = jnp.where((lane % side) != side - 1, moved, 0.0)
            at = (2 * sy + sx) * out_chan
            scr[at : at + out_chan, :] = moved.astype(BF16)


def low_kernel(
    grad_ref, back_ref, slope_ref, p1_ref, cells_ref, rows_ref, in_one_ref, done_ref,
    in_one_out, low_out, high_ref, scr,
):
    _, rows_pad, _ = p1_ref.shape
    part, _, width = rows_ref.shape
    extra = dot(rows_ref[...].reshape(part * rows_pad, width), cells_ref[...])
    p1 = [
        (extra[at * rows_pad : (at + 1) * rows_pad, :] + p1_ref[at].astype(F32)).astype(BF16) for at in range(part)
    ]
    shifted_up(grad_ref, scr)
    tall = high_ref.shape[0]
    hidden = tall // part
    grad_hidden = dot(back_ref[:, : scr.shape[0]], scr[...])
    high_ref[...] = grad_hidden[tall:, :]
    in_one = in_one_ref[...]
    total = jnp.zeros((hidden, rows_pad + hidden), F32)
    for block in range(part):
        rows = slice(block * hidden, (block + 1) * hidden)
        piece = (grad_hidden[rows, :] * slope_ref[rows, :]).astype(BF16)
        in_one += dot_nt(p1[block], p1[block])
        total += dot_nt(piece, jnp.concatenate([p1[block], piece], axis=0))
    in_one_out[...] = in_one
    low_out[...] = total


def high_kernel(
    above_ref, back_ref, high_ref, slope_ref, p1_ref, in_one_ref, low_ref, out_ref, scr,
):
    shifted_up(above_ref, scr)
    blocks, rows_pad, _ = p1_ref.shape
    part = blocks // 2
    tall, reach = high_ref.shape[0], scr.shape[0]
    hidden = tall // part
    grad_hidden = high_ref[...] + dot(back_ref[tall:, reach:], scr[...])
    total = low_ref[...]
    for block in range(part):
        rows = slice(block * hidden, (block + 1) * hidden)
        piece = (grad_hidden[rows, :] * slope_ref[rows, :]).astype(BF16)
        total += dot_nt(piece, jnp.concatenate([p1_ref[part + block], piece], axis=0))
    weight_one, out_one = total[:, :rows_pad], total[:, rows_pad:]
    out_ref[...] = pack_small(in_one_ref[...], weight_one, out_one).astype(BF16)


SMALL_DIAGONAL = 108
SMALL_WEIGHT = 64
SMALL_REST = 112


def pack_small(in_one, weight_one, out_one):
    row, col = square_iotas()
    hidden = weight_one.shape[0]
    half = hidden // 2
    wide = padded_lanes(weight_one)
    out_square = square(out_one)
    block = jnp.where(row <= col, square(in_one), jnp.where(row < hidden, out_square, 0.0))
    block = jnp.where(row == SMALL_DIAGONAL, diagonal_row(out_square), block)
    first = jnp.pad(wide, ((SMALL_WEIGHT, LANES - SMALL_WEIGHT - hidden), (0, 0)))
    block = jnp.where((row >= SMALL_WEIGHT) & (row < SMALL_WEIGHT + hidden) & (col < SMALL_WEIGHT), first, block)
    turned = pltpu.roll(wide[half:, :], LANES - SMALL_WEIGHT, axis=1)
    lane = lax.broadcasted_iota(jnp.int32, (half, LANES), 1)
    rest = jnp.where(lane >= SMALL_WEIGHT, wide[:half, :], turned)
    return jnp.where(row >= SMALL_REST, jnp.pad(rest, ((SMALL_REST, 0), (0, 0))), block)


def unpack_small(block, rows_one, hidden):
    half = hidden // 2
    turned = block.T
    in_one = first_of(block, turned)[:rows_one, :rows_one]
    out_one = second_of(block, turned, block[SMALL_DIAGONAL : SMALL_DIAGONAL + 1, :])[:hidden, :hidden]
    rest = block[SMALL_REST:, :]
    lane = lax.broadcasted_iota(jnp.int32, (hidden, LANES), 1)
    high = jnp.concatenate([rest, pltpu.roll(rest, SMALL_WEIGHT, axis=1)], axis=0)
    weight_one = jnp.where(lane < SMALL_WEIGHT, block[SMALL_WEIGHT : SMALL_WEIGHT + hidden, :], high)
    return in_one, weight_one[:, :rows_one], out_one


def joined_kernel(mine_ref, came_ref, small_ref, *refs):
    feat_refs, out_ref = refs[:-1], refs[-1]
    owners = out_ref.shape[0]
    large, small = mine_ref.shape[0] // owners, small_ref.shape[0] // owners
    feat_rows = feat_refs[0].shape[1]
    for owner in range(owners):
        rows = slice(owner * large, (owner + 1) * large)
        out_ref[owner, :large, :] = (mine_ref[rows, :].astype(F32) + came_ref[rows, :].astype(F32)).astype(BF16)
        out_ref[owner, large : large + small, :] = small_ref[owner * small : (owner + 1) * small, :]
        for change, feat_ref in enumerate(feat_refs):
            start = large + small + change * feat_rows
            out_ref[owner, start : start + feat_rows, :] = feat_ref[owner]


def total_kernel(came_ref, out_ref, *feat_refs):
    owners, chunk = came_ref.shape[0], out_ref.shape[0]
    total = came_ref[0, :chunk, :].astype(F32)
    for owner in range(1, owners):
        total += came_ref[owner, :chunk, :].astype(F32)
    out_ref[...] = total.astype(BF16)
    for change, feat_ref in enumerate(feat_refs):
        rows = feat_ref.shape[1]
        start = chunk + change * rows
        for owner in range(owners):
            feat_ref[owner] = came_ref[owner, start : start + rows, :]


def pair_kernel(mine_ref, came_ref, out_ref):
    total = (mine_ref[...].astype(F32) + came_ref[...].astype(F32)).astype(BF16)
    for owner in range(out_ref.shape[0]):
        out_ref[owner] = total


def features_kernel(owned_rows, *refs):
    feat_refs, out_ref, scr = refs[:-2], refs[-2], refs[-1]
    owners, owned = out_ref.shape[1], out_ref.shape[2]
    members, rows, _ = feat_refs[0].shape
    cube = lax.axis_index("space") // members
    for change, feat_ref in enumerate(feat_refs):
        for member in range(members):
            start = pl.multiple_of(((cube ^ change) * members + member) * rows, 16)
            scr[pl.ds(start, rows), :] = feat_ref[member].astype(F32)
    for i in range(owned_rows):
        block = scr[pl.ds(i, owners, stride=rows), :]
        for m in range(LANES // owned):
            out_ref[m * owned_rows + i] = block[:, m * owned : (m + 1) * owned].astype(BF16)


def gathered_half(source_ref, half_scr):
    owners = source_ref.shape[0]
    tall = half_scr.shape[0] // owners
    for owner in range(owners):
        half_scr[owner * tall : (owner + 1) * tall, :] = source_ref[owner, :tall, :]


def unit_square():
    row, col = square_iotas()
    return jnp.where(row == col, 1.0, 0.0).astype(BF16)


def first_half_copies(middle, factor, out_ref, sems):
    rows_two, split = out_ref.shape[0], middle * LANES
    spots = [(slice(0, split), slice(split, rows_two)), (slice(split, rows_two), slice(0, split))]
    return [pltpu.make_async_copy(factor.at[spot], out_ref.at[spot], sems.at[at]) for at, spot in enumerate(spots)]


def second_half_copies(middle, factor, out_ref, sems):
    rows_two, split = out_ref.shape[0], middle * LANES
    spots = [(slice(0, split), slice(0, split)), (slice(split, rows_two), slice(split, rows_two))]
    return [pltpu.make_async_copy(factor.at[spot], out_ref.at[spot], sems.at[at]) for at, spot in enumerate(spots)]


def wait_for(copies):
    for copy in copies:
        copy.wait()


def write_first_half(places, panels, middle, scale, half_scr, factor, out_ref, sems):
    copies = first_half_copies(middle, factor, out_ref, sems)
    rows_two = out_ref.shape[0]
    split = middle * LANES
    unit = unit_square()
    for j in range(middle, panels):
        wide = min(LANES, rows_two - j * LANES)
        start = places["block", 0, j]
        panel = half_scr[start : start + split, :]
        columns = slice(j * LANES, j * LANES + wide)
        factor[:split, columns] = (panel.astype(F32) * scale)[:, :wide]
        factor[columns, :split] = (dot_nt(unit, panel) * scale)[:wide, :]
    for copy in copies:
        copy.start()


def write_second_half(places, panels, middle, scale, half_scr, factor, out_ref, sems):
    copies = second_half_copies(middle, factor, out_ref, sems)
    rows_two = out_ref.shape[0]
    half = half_scr.shape[0]
    unit = unit_square()
    used = rows_two - (panels - 1) * LANES
    pairs = (panels + 1) // 2
    start = places["pair", pairs - 1] - half
    holder = half_scr[start : start + LANES, :].astype(F32)
    for j in range(panels):
        first = middle if j >= middle else 0
        if j == middle:
            copies[0].start()
        if j % 2 == 0:
            start = places["pair", j // 2] - half
            block = half_scr[start : start + LANES, :]
            turned = dot_nt(unit, block)
            block = block.astype(F32)
            wide = min(LANES, rows_two - j * LANES)
            rows = slice(j * LANES, j * LANES + wide)
            factor[rows, rows] = (first_of(block, turned) * scale)[:wide, :wide]
            if j + 1 < panels:
                rows = slice((j + 1) * LANES, (j + 2) * LANES)
                diagonal = holder[used + j // 2 : used + j // 2 + 1, :]
                factor[rows, rows] = second_of(block, turned, diagonal) * scale
        if j == first:
            continue
        wide = min(LANES, rows_two - j * LANES)
        start = places["block", first, j] - half
        panel = half_scr[start : start + (j - first) * LANES, :]
        columns, rows = slice(j * LANES, j * LANES + wide), slice(first * LANES, j * LANES)
        factor[rows, columns] = (panel.astype(F32) * scale)[:, :wide]
        factor[columns, rows] = (dot_nt(unit, panel) * scale)[:wide, :]
    copies[1].start()


def own_half_kernel(places, panels, middle, scale, mine_ref, out_ref, half_scr, factor, sems):
    gathered_half(mine_ref, half_scr)
    core = lax.axis_index("batch")
    rest = (places, panels, middle, scale, half_scr, factor, out_ref, sems)
    pl.when(core == 0)(functools.partial(write_first_half, *rest))
    pl.when(core == 1)(functools.partial(write_second_half, *rest))
    where = (middle, factor, out_ref, sems)
    pl.when(core == 0)(lambda: wait_for(first_half_copies(*where)))
    pl.when(core == 1)(lambda: wait_for(second_half_copies(*where)))


def unpack_kernel(
    places, panels, middle, scale_one, scale_two, begun_ref, mine_ref, came_ref,
    in_one_out, in_two_ref, out_one_out, out_two_out, weight_one_out, weight_two_out,
    packed, small, factor, in_one_ref, out_one_ref, out_two_ref, weight_one_ref, weight_two_ref, sems,
):
    core = lax.axis_index("batch")
    gathered_half(mine_ref, packed.at[core])
    gathered_half(came_ref, packed.at[1 - core])
    rest = (places, panels, middle, scale_two)
    pl.when(core == 1)(functools.partial(write_first_half, *rest, packed.at[0], factor, in_two_ref, sems))
    pl.when(core == 0)(functools.partial(write_second_half, *rest, packed.at[1], factor, in_two_ref, sems))
    out_chan, rows_two = weight_two_ref.shape
    hidden, rows_one = weight_one_ref.shape
    owners = mine_ref.shape[0]
    tall_large, tall_small = packed.shape[1] // owners, small.shape[0] // owners
    for owner in range(owners):
        rows = slice(tall_large, tall_large + tall_small)
        small[owner * tall_small : (owner + 1) * tall_small, :] = mine_ref[owner, rows, :].astype(F32) + came_ref[
            owner, rows, :
        ].astype(F32)
    half = packed.shape[1]

    def get(name, count):
        side, row = divmod(places[name], half)
        return packed[side, row : row + count, :].astype(F32)

    used = rows_two - (panels - 1) * LANES
    spare = LANES - used
    lane = lax.broadcasted_iota(jnp.int32, (1, LANES), 1)
    last = jnp.zeros((out_chan, LANES), F32)
    for i in range(-(-used // spare)):
        piece = pltpu.roll(get(("block", i, panels - 1), out_chan), LANES - (used - i * spare), axis=1)
        last = jnp.where((lane >= i * spare) & (lane < (i + 1) * spare), piece, last)
    for j in range(panels - 1):
        weight_two_ref[:, j * LANES : (j + 1) * LANES] = get(("weight_two", j), out_chan)
    weight_two_ref[:, (panels - 1) * LANES :] = last[:, :used]
    copies = [pltpu.make_async_copy(weight_two_ref, weight_two_out, sems.at[2])]
    copies[0].start()
    pairs = (panels + 1) // 2
    block = get(("pair", pairs - 1), LANES)
    diagonal = block[used + pairs - 1 : used + pairs, :]
    out_two_ref[...] = second_of(block, block.T, diagonal)[:out_chan, :out_chan]
    in_one, weight_one, out_one = unpack_small(small[...], rows_one, hidden)
    in_one_ref[...] = in_one * scale_one
    weight_one_ref[...] = weight_one
    out_one_ref[...] = out_one
    results = ((in_one_ref, in_one_out), (out_one_ref, out_one_out), (out_two_ref, out_two_out))
    for at, (here, there) in enumerate(results + ((weight_one_ref, weight_one_out),)):
        copies.append(pltpu.make_async_copy(here, there, sems.at[3 + at]))
        copies[-1].start()
    wait_for(copies)
    where = (middle, factor, in_two_ref, sems)
    pl.when(core == 1)(lambda: wait_for(first_half_copies(*where)))
    pl.when(core == 0)(lambda: wait_for(second_half_copies(*where)))


def cube_size(space):
    return 8 if space % 8 == 0 else space


def exchange(parts, size):
    space = lax.axis_size("space")
    groups = [list(range(base, base + size)) for base in range(0, space, size)]
    return lax.all_to_all(parts, "space", split_axis=0, concat_axis=0, axis_index_groups=groups)


def from_partner(block, stride):
    return lax.ppermute(block, "space", [(i, i ^ stride) for i in range(lax.axis_size("space"))])


def call(kernel, out_shape, scratch=(), micros=3, mib=24, **more):
    return pl.pallas_call(
        kernel,
        out_shape=out_shape,
        scratch_shapes=list(scratch),
        cost_estimate=pl.CostEstimate(flops=int(micros * 1.1e9), bytes_accessed=1 << 20, transcendentals=0),
        compiler_params=pltpu.CompilerParams(vmem_limit_bytes=mib * MIB),
        **more,
    )


def passed_along(block, axis, distance):
    devices = range(lax.axis_size(axis))
    route = [(i - distance, i) for i in devices if i - distance in devices]
    return lax.ppermute(block, axis, route)


def swapped(block):
    return lax.ppermute(block, "batch", [(0, 1), (1, 0)])


def like(shape, kind=BF16):
    return jax.ShapeDtypeStruct(shape, kind)


def split_scratch(count, plane):
    return [
        pltpu.VMEM((count * (plane + 8), plane), F32),
        pltpu.VMEM((count * 40, 4 * plane), BF16),
        pltpu.VMEM((8 * up_to(25 * count, 16), LANES), F32),
    ]


def local(volume, kernel_one, kernel_two, cotangent):
    channels, _, own, plane, _ = volume.shape
    rows_one, hidden = kernel_one.shape
    rows_two, out_chan = kernel_two.shape
    cells = cotangent.shape[3]
    side = math.isqrt(cells)
    space = lax.axis_size("space")
    devices_all = space * lax.axis_size("batch")
    total_one = devices_all * 8 * cells
    total_two = devices_all * cells
    rows_pad = up_to(rows_one, 16)
    halo = own - 1
    halo_width = up_to(25 * channels * halo, 16)
    own_width = up_to(25 * channels * own, 16)
    tall = 4 * hidden

    vol = volume.reshape(channels, own, plane, plane)
    halo_block = passed_along(vol[:, own - halo :], "space", 1)
    halo_rows = jnp.asarray(patch_rows(channels, 0, halo, (0, 1), rows_pad), BF16)
    own_rows = jnp.asarray(patch_rows(channels, halo, own, (1, 2), rows_pad), BF16)
    split = jnp.asarray(split_columns(plane, side), BF16)
    halo_wide, own_wide, back = call(
        prepare_kernel,
        (like((2 * tall, halo_width)), like((2 * tall, own_width)), like((2 * tall, 8 * out_chan))),
        [pltpu.VMEM((rows_two, LANES), F32)],
        micros=3,
    )(kernel_one.T, kernel_two.T, halo_rows, own_rows)
    part, act_high, slope_high, p1, in_one_part = call(
        own_kernel,
        (
            like((tall, cells), F32),
            like((tall, cells), F32),
            like((tall, cells), F32),
            like((8, rows_pad, cells)),
            like((rows_pad, rows_pad), F32),
        ),
        split_scratch(channels * own, plane) + [pltpu.VMEM((own_width, cells), BF16)],
        micros=6,
    )(vol, own_wide, split, own_rows)
    panels, middle, places, large_rows = large_places(rows_two, out_chan)
    feat_rows = out_chan * cells // space // LANES
    feat_tall = up_to(feat_rows, 16)
    cube = cube_size(space)
    cubes = space // cube
    grad_two, p2, slope_low, spread, *feats = call(
        functools.partial(forward_kernel, 1.0 / math.sqrt(total_two)),
        (
            like((out_chan, cells)),
            like((panels * LANES, cells)),
            like((tall, cells), F32),
            like((halo_width, cells)),
        )
        + (like((cube, feat_tall, LANES)),) * cubes,
        split_scratch(channels * halo, plane)
        + [pltpu.VMEM((rows_two * (cells // LANES), LANES), F32), pltpu.VMEM((space, feat_tall, LANES), BF16)],
        micros=5,
    )(halo_block, halo_wide, split, part, act_high, kernel_two.T, cotangent.reshape(out_chan, cells))
    above = passed_along(grad_two, "space", -1)

    half = large_rows // 2
    small_rows = LANES
    chunk = (half + small_rows) // cube
    mine, other, done = call(
        functools.partial(sums_kernel, places, rows_two),
        (like((half, LANES)), like((half, LANES)), like((8, LANES), F32)),
        [
            pltpu.VMEM((2, half, LANES), BF16),
            pltpu.VMEM((2, panels * LANES, 2 * LANES), F32),
            pltpu.SemaphoreType.DMA((2,)),
        ],
        micros=5,
        out_specs=tuple(pl.BlockSpec(memory_space=pl.ANY if at < 2 else pltpu.VMEM) for at in range(3)),
    )(p2, grad_two)
    came = swapped(other)
    in_one_low, low, high = call(
        low_kernel,
        (like((rows_pad, rows_pad), F32), like((hidden, rows_pad + hidden), F32), like((tall, cells), F32)),
        [pltpu.VMEM((4 * out_chan, cells), BF16)],
        micros=0.1,
    )(grad_two, back, slope_low, p1, spread, halo_rows[4:], in_one_part, done)
    small = call(
        high_kernel,
        like((small_rows, LANES)),
        [pltpu.VMEM((4 * out_chan, cells), BF16)],
        micros=12,
    )(above, back, high, slope_high, p1, in_one_low, low)
    joined = call(joined_kernel, like((cube, chunk + cubes * feat_tall, LANES)), micros=1)(mine, came, small, *feats)
    total, *feats = call(
        total_kernel, (like((chunk, LANES)),) + (like((cube, feat_tall, LANES)),) * cubes, micros=1
    )(exchange(joined, cube))
    stride = cube
    while 2 * stride < space:
        total = (total.astype(F32) + from_partner(total, stride).astype(F32)).astype(BF16)
        stride *= 2
    other = from_partner(total, stride) if stride < space else jnp.zeros_like(total)
    copies = call(pair_kernel, like((cube, chunk, LANES)), micros=1)(total, other)
    mine = exchange(copies, cube)
    feats[1:] = [from_partner(feats[change], change * cube) for change in range(1, cubes)]
    mine, feats = lax.optimization_barrier((mine, feats))
    came = swapped(mine)
    features = call(
        functools.partial(features_kernel, feat_rows),
        like((out_chan, space, cells // space)),
        [pltpu.VMEM((space * feat_tall, LANES), F32)],
        micros=1,
    )(*feats)
    anywhere = pl.BlockSpec(memory_space=pl.ANY)
    begun = call(
        functools.partial(own_half_kernel, places, panels, middle, 1.0 / total_two),
        like((rows_two, rows_two), F32),
        [
            pltpu.VMEM((half, LANES), BF16),
            pltpu.VMEM((rows_two, rows_two), F32),
            pltpu.SemaphoreType.DMA((2,)),
        ],
        micros=2,
        out_specs=anywhere,
    )(mine)
    kinds = [
        like(shape, F32)
        for shape in (
            (rows_one, rows_one),
            (rows_two, rows_two),
            (hidden, hidden),
            (out_chan, out_chan),
            (hidden, rows_one),
            (out_chan, rows_two),
        )
    ]
    in_one, in_two, out_one, out_two, weight_one, weight_two = call(
        functools.partial(unpack_kernel, places, panels, middle, 1.0 / total_one, 1.0 / total_two),
        tuple(kinds),
        [
            pltpu.VMEM((2, half, LANES), BF16),
            pltpu.VMEM((small_rows, LANES), F32),
            pltpu.VMEM((rows_two, rows_two), F32),
        ]
        + [pltpu.VMEM(kind.shape, F32) for at, kind in enumerate(kinds) if at != 1]
        + [pltpu.SemaphoreType.DMA((7,))],
        micros=2,
        in_specs=[anywhere, pl.BlockSpec(memory_space=pltpu.VMEM), pl.BlockSpec(memory_space=pltpu.VMEM)],
        out_specs=(anywhere,) * 6,
        input_output_aliases={0: 1},
    )(begun, mine, came)
    features = features.reshape(out_chan, 1, space, cells // space)
    return features, in_one, in_two, out_one, out_two, weight_one.T, weight_two.T


def solution(mesh):
    placed = (P(None, "batch", "space", None, None), P(), P(), P(None, "batch", "space", None))
    return jax.shard_map(
        local,
        mesh=mesh,
        in_specs=placed,
        out_specs=(P(None, "batch", None, "space"), P(), P(), P(), P(), P(), P()),
        check_vma=False,
    )
```

profile of v0, /device:TPU:0, one launch (start us, length us, event | category | flops | bytes accessed | tf_op | source)
XLA Modules:
  0.0 65.5 jit_solution(5580408868749759213)
XLA Ops:
  0.6 1.0 %slice.8 = bf16[4,3,128,128]{3,2,1,0:T(8,128)(2,1)S(1)} slice(bf16[4,4,128,128]{3,2,1,0:T(8,128)(2,1)} %bitcast.9), slice={[0:4], [1:4], [0:128], [0:128]} | slice | bytes 786432 | tf_op jit(solution)/shard_map/slice | solution.py:706
  1.7 4.9 %collective-permute-start = (bf16[4,3,128,128]{3,2,1,0:T(8,128)(2,1)S(1)}, bf16[4,3,128,128]{3,2,1,0:T(8,128)(2,1)S(1)}, u32[]{:S(2)}, u32[]{:S(2)}) collective-permute-start(bf16[4,3,128,128]{3,2,1,0:T(8,128)(2,1)S(1)} %slice.8), channel_id=1, source_target_pairs={{0,2},{2,4},{4,6},{6,8},{8,10},{10,12},{12,14},{14,16},{16,18},{18... | collective-permute-start | bytes 1179656 | tf_op jit(solution)/shard_map/ppermute | solution.py:670
  6.6 0.9 %copy-done.3 = bf16[864,64]{0,1:T(8,128)(2,1)S(1)} copy-done((bf16[864,64]{0,1:T(8,128)(2,1)S(1)}, bf16[864,64]{0,1:T(8,128)(2,1)}, u32[]{:S(2)}) %copy-start.3) | copy-done | bytes 110616
  7.4 0.7 %copy-done.5 = bf16[108,32]{0,1:T(8,128)(2,1)S(1)} copy-done((bf16[108,32]{0,1:T(8,128)(2,1)S(1)}, bf16[108,32]{0,1:T(8,128)(2,1)}, u32[]{:S(2)}) %copy-start.5) | copy-done | bytes 6936
  8.1 1.2 %copy-done.6 = bf16[8,112,400]{2,1,0:T(8,128)(2,1)S(1)} copy-done((bf16[8,112,400]{2,1,0:T(8,128)(2,1)S(1)}, bf16[8,112,400]{2,1,0:T(8,128)(2,1)}, u32[]{:S(2)}) %copy-start.6) | copy-done | bytes 716824
  9.3 1.1 %copy-done.8 = bf16[8,112,304]{2,1,0:T(8,128)(2,1)S(1)} copy-done((bf16[8,112,304]{2,1,0:T(8,128)(2,1)S(1)}, bf16[8,112,304]{2,1,0:T(8,128)(2,1)}, u32[]{:S(2)}) %copy-start.8) | copy-done | bytes 544792
  10.4 0.4 shard_map.126
  10.8 0.7 %copy-done.1 = bf16[4,1,4,128,128]{4,3,2,1,0:T(8,128)(2,1)S(1)} copy-done((bf16[4,1,4,128,128]{4,3,2,1,0:T(8,128)(2,1)S(1)}, bf16[4,1,4,128,128]{4,3,2,1,0:T(8,128)(2,1)}, u32[]{:S(2)}) %copy-start.1) | copy-done | bytes 524312
  11.5 0.3 copy-done.7
  11.8 0.2 copy-done.9
  11.9 3.2 %shard_map.127 = (f32[128,1024]{1,0:T(8,128)S(1)}, f32[128,1024]{1,0:T(8,128)S(1)}, f32[128,1024]{1,0:T(8,128)S(1)}, bf16[8,112,1024]{2,1,0:T(8,128)(2,1)S(1)}, f32[112,112]{1,0:T(8,128)S(1)}) custom-call(bf16[4,4,128,128]{3,2,1,0:T(8,128)(2,1)S(1)} %bitcast.10, bf16[256,400]{1,0:T(8,128)(2,1)S(1)} %get-tuple-element.40.wide_ref, ...), custom_call_target="tpu_custom_call" | custom-call | flops 6600000000 | bytes 1048576 | tf_op jit(solution)/shard_map/pallas_call | solution.py:716
  15.2 2.5 %shard_map.128 = (bf16[64,1024]{1,0:T(8,128)(2,1)S(1)}, bf16[896,1024]{1,0:T(8,128)(2,1)S(1)}, f32[128,1024]{1,0:T(8,128)S(1)}, bf16[304,1024]{1,0:T(8,128)(2,1)...) custom-call(bf16[4,3,128,128]{3,2,1,0:T(8,128)(2,1)S(1)} %collective-permute-done.halo_ref, ...), custom_call_target="tpu_custom_call" | custom-call | flops 5500000256 | bytes 1048576 | tf_op jit(solution)/shard_map/pallas_call | solution.py:733
  17.7 1.3 %collective-permute-start.2 = (bf16[64,1024]{1,0:T(8,128)(2,1)S(1)}, bf16[64,1024]{1,0:T(8,128)(2,1)S(1)}, u32[]{:S(2)}, u32[]{:S(2)}) collective-permute-start(bf16[64,1024]{1,0:T(8,128)(2,1)S(1)} %get-tuple-element.44.grad_ref), channel_id=1, source_target_pairs={{2,0},{4,2},{6,4},{8,6},{10,8},{12,10},{14,12},{16,14},{18,16},{20... | collective-permute-start | bytes 393224 | tf_op jit(solution)/shard_map/ppermute | solution.py:670
  19.0 0.0 copy-start
  19.0 2.6 %shard_map.129 = (bf16[1792,128]{1,0:T(8,128)(2,1)S(1)}, bf16[1792,128]{1,0:T(8,128)(2,1)S(1)}, f32[8,128]{1,0:T(8,128)S(1)}) custom-call(bf16[896,1024]{1,0:T(8,128)(2,1)S(1)} %get-tuple-element.43.p2_ref, bf16[64,1024]{1,0:T(8,128)(2,1)S(1)} %get-tuple-element.44.grad_ref), custom_call_target="tpu_custom_call" | custom-call | flops 5500000256 | bytes 1048576 | tf_op jit(solution)/shard_map/pallas_call | solution.py:751
  21.7 0.1 collective-permute-start.1
  21.7 1.4 %shard_map.130 = (f32[112,112]{1,0:T(8,128)S(1)}, f32[32,144]{1,0:T(8,128)S(1)}, f32[128,1024]{1,0:T(8,128)S(1)}) custom-call(bf16[64,1024]{1,0:T(8,128)(2,1)S(1)} %get-tuple-element.44.grad_ref, bf16[256,512]{1,0:T(8,128)(2,1)S(1)} %get-tuple-element.47.back_ref, f32[128,1024]{1,0:T(8,128)S(1)} %get-tuple-element.48.slope_ref, ...), custom_call_target="tpu_custom_call" | custom-call | flops 110000000 | bytes 1048576 | tf_op jit(solution)/shard_map/pallas_call | solution.py:763
  23.2 1.6 %collective-permute-done.2.above_ref = bf16[64,1024]{1,0:T(8,128)(2,1)S(1)} collective-permute-done((bf16[64,1024]{1,0:T(8,128)(2,1)S(1)}, bf16[64,1024]{1,0:T(8,128)(2,1)S(1)}, u32[]{:S(2)}, u32[]{:S(2)}) %collective-permute-start.2) | collective-permute-done | bytes 131104 | tf_op jit(solution)/shard_map/ppermute | solution.py:670
  24.7 0.7 %shard_map.131.small_ref = bf16[128,128]{1,0:T(8,128)(2,1)S(1)} custom-call(bf16[64,1024]{1,0:T(8,128)(2,1)S(1)} %collective-permute-done.2.above_ref, bf16[256,512]{1,0:T(8,128)(2,1)S(1)} %get-tuple-element.47.back_ref, f32[128,1024]{1,0:T(8,128)S(1)} %get-tuple-element.53.high_ref, f32[128,1024]{1,0:T(8,128)S(1)} %get-tuple-element.54.slope_ref, ...), custom_call_target="tpu_custom_call" | custom-call | flops 13200000000 | bytes 1048576 | tf_op jit(solution)/shard_map/pallas_call | solution.py:769
  25.5 0.1 shard_map.132
  25.6 17.1 %all_to_all.10.came_ref = bf16[8,304,128]{2,1,0:T(8,128)(2,1)S(1)} all-to-all(bf16[8,304,128]{2,1,0:T(8,128)(2,1)S(1)} %shard_map.132), channel_id=1, replica_groups={{0,2,4,6,8,10,12,14},{16,18,20,22,24,26,28,30},{1,3,5,7,9,11,13,15},{17..., dimensions={0} | all-to-all | bytes 1245184 | tf_op jit(solution)/shard_map/all_to_all | solution.py:649
  42.7 0.1 shard_map.133
  42.8 2.7 %collective-permute-start.3 = (bf16[240,128]{1,0:T(8,128)(2,1)S(1)}, bf16[240,128]{1,0:T(8,128)(2,1)S(1)}, u32[]{:S(2)}, u32[]{:S(2)}) collective-permute-start(bf16[240,128]{1,0:T(8,128)(2,1)S(1)} %get-tuple-element.59.mine_ref), channel_id=1, source_target_pairs={{0,16},{2,18},{4,20},{6,22},{8,24},{10,26},{12,28},{14,30},{16,0},... | collective-permute-start | bytes 184328 | tf_op jit(solution)/shard_map/ppermute | solution.py:653
  45.4 3.2 %collective-permute-done.3.came_ref = bf16[240,128]{1,0:T(8,128)(2,1)S(1)} collective-permute-done((bf16[240,128]{1,0:T(8,128)(2,1)S(1)}, bf16[240,128]{1,0:T(8,128)(2,1)S(1)}, u32[]{:S(2)}, u32[]{:S(2)}) %collective-permute-start.3) | collective-permute-done | bytes 61472 | tf_op jit(solution)/shard_map/ppermute | solution.py:653
  48.6 0.8 %shard_map.134 = bf16[8,240,128]{2,1,0:T(8,128)(2,1)} custom-call(bf16[240,128]{1,0:T(8,128)(2,1)S(1)} %get-tuple-element.59.mine_ref, bf16[240,128]{1,0:T(8,128)(2,1)S(1)} %collective-permute-done.3.came_ref), custom_call_target="tpu_custom_call" | custom-call | flops 1100000000 | bytes 1048576 | tf_op jit(solution)/shard_map/pallas_call | solution.py:784
  49.5 3.5 %all-to-all-start.1 = ((bf16[8,240,128]{2,1,0:T(8,128)(2,1)}), bf16[8,240,128]{2,1,0:T(8,128)(2,1)S(1)}, u32[]{:S(2)}, u32[]{:S(2)}) async-start(bf16[8,240,128]{2,1,0:T(8,128)(2,1)} %shard_map.134), calls=%async_computation.1 | async-start | bytes 983040 | tf_op jit(solution)/shard_map/all_to_all | solution.py:649
  52.9 2.0 %collective-permute-start.4 = (bf16[8,32,128]{2,1,0:T(8,128)(2,1)S(1)}, bf16[8,32,128]{2,1,0:T(8,128)(2,1)S(1)}, u32[]{:S(2)}, u32[]{:S(2)}) collective-permute-start(bf16[8,32,128]{2,1,0:T(8,128)(2,1)S(1)} %get-tuple-element.61), channel_id=1, source_target_pairs={{0,16},{2,18},{4,20},{6,22},{8,24},{10,26},{12,28},{14,30},{16,0},... | collective-permute-start | bytes 196616 | tf_op jit(solution)/shard_map/ppermute | solution.py:653
  54.9 3.9 %collective-permute-done.4.refs_1_ = bf16[8,32,128]{2,1,0:T(8,128)(2,1)S(1)} collective-permute-done((bf16[8,32,128]{2,1,0:T(8,128)(2,1)S(1)}, bf16[8,32,128]{2,1,0:T(8,128)(2,1)S(1)}, u32[]{:S(2)}, u32[]{:S(2)}) %collective-permute-start.4) | collective-permute-done | bytes 65568 | tf_op jit(solution)/shard_map/ppermute | solution.py:653
  58.9 2.6 %all-to-all-done.1.mine_ref = bf16[8,240,128]{2,1,0:T(8,128)(2,1)S(1)} async-done(((bf16[8,240,128]{2,1,0:T(8,128)(2,1)}), bf16[8,240,128]{2,1,0:T(8,128)(2,1)S(1)}, u32[]{:S(2)}, u32[]{:S(2)}) %all-to-all-start.1) | async-done | bytes 491552 | tf_op jit(solution)/shard_map/all_to_all | solution.py:649
  61.4 1.0 %shard_map.135 = bf16[64,16,64]{2,1,0:T(8,128)(2,1)} custom-call(bf16[8,32,128]{2,1,0:T(8,128)(2,1)S(1)} %get-tuple-element.62.refs_0_, bf16[8,32,128]{2,1,0:T(8,128)(2,1)S(1)} %collective-permute-done.4.refs_1_), custom_call_target="tpu_custom_call" | custom-call | flops 1100000000 | bytes 1048576 | tf_op jit(solution)/shard_map/pallas_call | solution.py:789
  62.4 1.4 %shard_map.136.begun_ref = f32[864,864]{1,0:T(8,128)} custom-call(bf16[8,240,128]{2,1,0:T(8,128)(2,1)S(1)} %all-to-all-done.1.mine_ref), custom_call_target="tpu_custom_call" | custom-call | flops 2200000000 | bytes 1048576 | tf_op jit(solution)/shard_map/pallas_call | solution.py:796
  63.9 1.7 %shard_map.137 = (f32[108,108]{1,0:T(8,128)}, f32[864,864]{1,0:T(8,128)}, f32[32,32]{1,0:T(8,128)}, f32[64,64]{1,0:T(8,128)}, f32[32,108]{1,0:T(8,128)}, /*index=5*/f32[64,864]{1,0:T(8,128)}) custom-call(f32[864,864]{1,0:T(8,128)} %shard_map.136.begun_ref, bf16[8,240,128]{2,1,0:T(8,128)(2,1)S(1)} %all-to-all-done.1.mine_ref, ...), custom_call_target="tpu_custom_call", output_to_operand_aliasing={{1}: (0, {})} | custom-call | flops 2200000000 | bytes 1048576 | tf_op jit(solution)/shard_map/pallas_call | solution.py:818
  (16 shorter events, 0.0 us)
Async XLA Ops:
  1.7 13.5 %collective-permute-start = (bf16[4,3,128,128]{3,2,1,0:T(8,128)(2,1)S(1)}, bf16[4,3,128,128]{3,2,1,0:T(8,128)(2,1)S(1)}, u32[]{:S(2)}, u32[]{:S(2)}) collective-permute-start(bf16[4,3,128,128]{3,2,1,0:T(8,128)(2,1)S(1)} %slice.8), channel_id=1, source_target_pairs={{0,2},{2,4},{4,6},{6,8},{8,10},{10,12},{12,14},{14,16},{16,18},{18... | collective-permute-start | bytes 1179656 | tf_op jit(solution)/shard_map/ppermute | solution.py:670
  6.5 0.9 %copy-start.3 = (bf16[864,64]{0,1:T(8,128)(2,1)S(1)}, bf16[864,64]{0,1:T(8,128)(2,1)}, u32[]{:S(2)}) copy-start(bf16[864,64]{0,1:T(8,128)(2,1)} %param.9) | copy-start | bytes 331780
  7.4 0.7 %copy-start.5 = (bf16[108,32]{0,1:T(8,128)(2,1)S(1)}, bf16[108,32]{0,1:T(8,128)(2,1)}, u32[]{:S(2)}) copy-start(bf16[108,32]{0,1:T(8,128)(2,1)} %param.8) | copy-start | bytes 20740
  8.1 1.2 %copy-start.6 = (bf16[8,112,400]{2,1,0:T(8,128)(2,1)S(1)}, bf16[8,112,400]{2,1,0:T(8,128)(2,1)}, u32[]{:S(2)}) copy-start(bf16[8,112,400]{2,1,0:T(8,128)(2,1)} %constant.7.clone.own_rows_ref.rows_ref) | copy-start | bytes 2150404
  9.3 1.1 %copy-start.8 = (bf16[8,112,304]{2,1,0:T(8,128)(2,1)S(1)}, bf16[8,112,304]{2,1,0:T(8,128)(2,1)}, u32[]{:S(2)}) copy-start(bf16[8,112,304]{2,1,0:T(8,128)(2,1)} %constant.6.clone.halo_rows_ref) | copy-start | bytes 1634308
  10.4 1.0 %copy-start.1 = (bf16[4,1,4,128,128]{4,3,2,1,0:T(8,128)(2,1)S(1)}, bf16[4,1,4,128,128]{4,3,2,1,0:T(8,128)(2,1)}, u32[]{:S(2)}) copy-start(bf16[4,1,4,128,128]{4,3,2,1,0:T(8,128)(2,1)} %param.7) | copy-start | bytes 1572868
  10.4 1.3 %copy-start.7 = (bf16[8,112,400]{2,1,0:T(8,128)(2,1)S(1)}, bf16[8,112,400]{2,1,0:T(8,128)(2,1)}, u32[]{:S(2)}) copy-start(bf16[8,112,400]{2,1,0:T(8,128)(2,1)} %constant.7.clone.own_rows_ref.rows_ref) | copy-start | bytes 2150404
  10.4 1.5 %copy-start.9 = (bf16[512,640]{1,0:T(8,128)(2,1)S(1)}, bf16[512,640]{1,0:T(8,128)(2,1)}, u32[]{:S(2)}) copy-start(bf16[512,640]{1,0:T(8,128)(2,1)} %constant.8.clone.split_ref) | copy-start | bytes 1966084
  11.9 3.2 %copy-start.2 = (bf16[64,1,1,1024]{3,0,2,1:T(8,128)(2,1)S(1)}, bf16[64,1,1,1024]{3,0,2,1:T(8,128)(2,1)}, u32[]{:S(2)}) copy-start(bf16[64,1,1,1024]{3,0,2,1:T(8,128)(2,1)} %param.10) | copy-start | bytes 393220
  11.9 3.2 %copy-start.4 = (bf16[864,64]{0,1:T(8,128)(2,1)S(1)}, bf16[864,64]{0,1:T(8,128)(2,1)}, u32[]{:S(2)}) copy-start(bf16[864,64]{0,1:T(8,128)(2,1)} %param.9) | copy-start | bytes 331780
  17.7 7.0 %collective-permute-start.2 = (bf16[64,1024]{1,0:T(8,128)(2,1)S(1)}, bf16[64,1024]{1,0:T(8,128)(2,1)S(1)}, u32[]{:S(2)}, u32[]{:S(2)}) collective-permute-start(bf16[64,1024]{1,0:T(8,128)(2,1)S(1)} %get-tuple-element.44.grad_ref), channel_id=1, source_target_pairs={{2,0},{4,2},{6,4},{8,6},{10,8},{12,10},{14,12},{16,14},{18,16},{20... | collective-permute-start | bytes 393224 | tf_op jit(solution)/shard_map/ppermute | solution.py:670
  19.0 2.7 %copy-start = (bf16[4,112,304]{2,1,0:T(8,128)(2,1)S(1)}, bf16[4,112,304]{2,1,0:T(8,128)(2,1)}, u32[]{:S(2)}) copy-start(bf16[4,112,304]{2,1,0:T(8,128)(2,1)} %constant.11.rows_ref) | copy-start | bytes 817156
  21.7 3.8 %collective-permute-start.1 = (bf16[1792,128]{1,0:T(8,128)(2,1)S(1)}, bf16[1792,128]{1,0:T(8,128)(2,1)S(1)}, u32[]{:S(2)}, u32[]{:S(2)}) collective-permute-start(bf16[1792,128]{1,0:T(8,128)(2,1)S(1)} %get-tuple-element.46), channel_id=1, source_target_pairs={{0,1},{1,0},{2,3},{3,2},{4,5},{5,4},{6,7},{7,6},{8,9},{9,8},{10,11... | collective-permute-start | bytes 1376264 | tf_op jit(solution)/shard_map/ppermute | solution.py:674
  42.8 5.8 %collective-permute-start.3 = (bf16[240,128]{1,0:T(8,128)(2,1)S(1)}, bf16[240,128]{1,0:T(8,128)(2,1)S(1)}, u32[]{:S(2)}, u32[]{:S(2)}) collective-permute-start(bf16[240,128]{1,0:T(8,128)(2,1)S(1)} %get-tuple-element.59.mine_ref), channel_id=1, source_target_pairs={{0,16},{2,18},{4,20},{6,22},{8,24},{10,26},{12,28},{14,30},{16,0},... | collective-permute-start | bytes 184328 | tf_op jit(solution)/shard_map/ppermute | solution.py:653
  49.5 12.0 %all-to-all-start.1 = ((bf16[8,240,128]{2,1,0:T(8,128)(2,1)}), bf16[8,240,128]{2,1,0:T(8,128)(2,1)S(1)}, u32[]{:S(2)}, u32[]{:S(2)}) async-start(bf16[8,240,128]{2,1,0:T(8,128)(2,1)} %shard_map.134), calls=%async_computation.1 | async-start | bytes 983040 | tf_op jit(solution)/shard_map/all_to_all | solution.py:649
  52.9 5.9 %collective-permute-start.4 = (bf16[8,32,128]{2,1,0:T(8,128)(2,1)S(1)}, bf16[8,32,128]{2,1,0:T(8,128)(2,1)S(1)}, u32[]{:S(2)}, u32[]{:S(2)}) collective-permute-start(bf16[8,32,128]{2,1,0:T(8,128)(2,1)S(1)} %get-tuple-element.61), channel_id=1, source_target_pairs={{0,16},{2,18},{4,20},{6,22},{8,24},{10,26},{12,28},{14,30},{16,0},... | collective-permute-start | bytes 196616 | tf_op jit(solution)/shard_map/ppermute | solution.py:653
  61.4 2.4 %collective-permute-start.5 = (bf16[8,240,128]{2,1,0:T(8,128)(2,1)S(1)}, bf16[8,240,128]{2,1,0:T(8,128)(2,1)S(1)}, u32[]{:S(2)}, u32[]{:S(2)}) collective-permute-start(bf16[8,240,128]{2,1,0:T(8,128)(2,1)S(1)} %all-to-all-done.1.mine_ref), channel_id=1, source_target_pairs={{0,1},{1,0},{2,3},{3,2},{4,5},{5,4},{6,7},{7,6},{8,9},{9,8},{10,11... | collective-permute-start | bytes 1474568 | tf_op jit(solution)/shard_map/ppermute | solution.py:674
where the time goes:
time: 66.1 us; the launch traced here: 65.5 us
  blocking collectives  17.1 us (26%)
  Pallas kernels  15.9 us (24%)
  starting transfers between devices  14.4 us (22%)
  waiting for transfers between devices  11.3 us (17%)
  local copies, waits for them, and re-layouts  6.06 us (9%)
  between operations  0.78 us (1%)
    all_to_all x1, blocking collectives, exchange(): lax.all_to_all(parts, 'space', split_axis=0, concat_axis=0, axis_index_gr...  17.1 us
    ppermute x2, waiting for transfers between devices, from_partner(): lax.ppermute(block, 'space', [(i, i ^ stride) for i in range(lax.axis_siz...  7.13 us
    ppermute x2, starting transfers between devices, passed_along(): return lax.ppermute(block, axis, route)  6.16 us
    unnamed x20, local copies, waits for them, and re-layouts  5.03 us
    ppermute x2, starting transfers between devices, from_partner(): lax.ppermute(block, 'space', [(i, i ^ stride) for i in range(lax.axis_siz...  4.65 us
    all_to_all x1, starting transfers between devices, exchange(): lax.all_to_all(parts, 'space', split_axis=0, concat_axis=0, axis_index_gr...  3.48 us
    pallas_call x1, Pallas kernels, local(): call(own_kernel, (like((tall, cells), F32), like((tall, cells), F32), lik...  3.17 us
    pallas_call x1, Pallas kernels, local(): call(functools.partial(sums_kernel, places, rows_two), (like((half, LANES...  2.64 us
  transfers between devices with their start and end apart: 7, of which 4 were waited for; matrix products, arithmetic and copies ran while one was open for 0% of the time, Pallas kernels for 16%

commit v1 on v0

--- a/solution.py
+++ b/solution.py
@@ -288,20 +288,27 @@
     return jnp.pad(block, ((0, 0), (0, LANES - block.shape[1])))
 
 
-def put(packed, at, block):
-    half = packed.shape[1]
+def put(halves, at, block):
+    half = halves[0].shape[0]
     done = 0
     while done < block.shape[0]:
         side, row = divmod(at + done, half)
         count = min(block.shape[0] - done, half - row)
-        packed[side, row : row + count, :] = block[done : done + count, :].astype(BF16)
+        halves[side][row : row + count, :] = block[done : done + count, :].astype(BF16)
         done += count
 
 
 def sums_kernel(
-    places, rows_two, p2_ref, grad_ref, mine_ref, other_ref, done_ref, packed, product_scr, sems,
+    places, rows_two, p2_ref, grad_ref, mine_ref, other_ref, done_ref, product_scr,
 ):
     done_ref[...] = jnp.zeros_like(done_ref)
+    core = lax.axis_index("batch")
+    rest = (places, rows_two, p2_ref, grad_ref, product_scr)
+    pl.when(core == 0)(lambda: write_sums(*rest, (mine_ref, other_ref)))
+    pl.when(core == 1)(lambda: write_sums(*rest, (other_ref, mine_ref)))
+
+
+def write_sums(places, rows_two, p2_ref, grad_ref, product_scr, packed):
     panels = p2_ref.shape[0] // LANES
     used = rows_two - (panels - 1) * LANES
     lane = lax.broadcasted_iota(jnp.int32, (1, LANES), 1)
@@ -338,13 +345,6 @@
         put(packed, places["pair", j // 2], block)
     for j in range(panels - 1):
         put(packed, places["weight_two", j], weight_two[:, j * LANES : (j + 1) * LANES])
-    core = lax.axis_index("batch")
-    mine = pltpu.make_async_copy(packed.at[core], mine_ref, sems.at[0])
-    other = pltpu.make_async_copy(packed.at[1 - core], other_ref, sems.at[1])
-    other.start()
-    mine.start()
-    other.wait()
-    mine.wait()
 
 
 def shifted_up(source, scr):
@@ -457,17 +457,14 @@
             out_ref[owner, start : start + feat_rows, :] = feat_ref[owner]
 
 
-def total_kernel(came_ref, out_ref, *feat_refs):
+def total_kernel(came_ref, out_ref, feat_ref):
     owners, chunk = came_ref.shape[0], out_ref.shape[0]
     total = came_ref[0, :chunk, :].astype(F32)
     for owner in range(1, owners):
         total += came_ref[owner, :chunk, :].astype(F32)
     out_ref[...] = total.astype(BF16)
-    for change, feat_ref in enumerate(feat_refs):
-        rows = feat_ref.shape[1]
-        start = chunk + change * rows
-        for owner in range(owners):
-            feat_ref[owner] = came_ref[owner, start : start + rows, :]
+    for owner in range(owners):
+        feat_ref[owner] = came_ref[owner, chunk:, :]
 
 
 def pair_kernel(mine_ref, came_ref, out_ref):
@@ -476,15 +473,15 @@
         out_ref[owner] = total
 
 
-def features_kernel(owned_rows, *refs):
-    feat_refs, out_ref, scr = refs[:-2], refs[-2], refs[-1]
+def features_kernel(owned_rows, cubes, feat_ref, out_ref, scr):
     owners, owned = out_ref.shape[1], out_ref.shape[2]
-    members, rows, _ = feat_refs[0].shape
+    rows = feat_ref.shape[1] // cubes
+    members = owners // cubes
     cube = lax.axis_index("space") // members
-    for change, feat_ref in enumerate(feat_refs):
+    for change in range(cubes):
         for member in range(members):
             start = pl.multiple_of(((cube ^ change) * members + member) * rows, 16)
-            scr[pl.ds(start, rows), :] = feat_ref[member].astype(F32)
+            scr[pl.ds(start, rows), :] = feat_ref[member, change * rows : (change + 1) * rows, :].astype(F32)
     for i in range(owned_rows):
         block = scr[pl.ds(i, owners, stride=rows), :]
         for m in range(LANES // owned):
@@ -743,7 +740,9 @@
         + [pltpu.VMEM((rows_two * (cells // LANES), LANES), F32), pltpu.VMEM((space, feat_tall, LANES), BF16)],
         micros=5,
     )(halo_block, halo_wide, split, part, act_high, kernel_two.T, cotangent.reshape(out_chan, cells))
+    feats = feats[:1] + [from_partner(feats[change], change * cube) for change in range(1, cubes)]
     above = passed_along(grad_two, "space", -1)
+    feats, above = lax.optimization_barrier((feats, above))
 
     half = large_rows // 2
     small_rows = LANES
@@ -751,13 +750,8 @@
     mine, other, done = call(
         functools.partial(sums_kernel, places, rows_two),
         (like((half, LANES)), like((half, LANES)), like((8, LANES), F32)),
-        [
-            pltpu.VMEM((2, half, LANES), BF16),
-            pltpu.VMEM((2, panels * LANES, 2 * LANES), F32),
-            pltpu.SemaphoreType.DMA((2,)),
-        ],
-        micros=5,
-        out_specs=tuple(pl.BlockSpec(memory_space=pl.ANY if at < 2 else pltpu.VMEM) for at in range(3)),
+        [pltpu.VMEM((2, panels * LANES, 2 * LANES), F32)],
+        micros=0.1,
     )(p2, grad_two)
     came = swapped(other)
     in_one_low, low, high = call(
@@ -773,25 +767,24 @@
         micros=12,
     )(above, back, high, slope_high, p1, in_one_low, low)
     joined = call(joined_kernel, like((cube, chunk + cubes * feat_tall, LANES)), micros=1)(mine, came, small, *feats)
-    total, *feats = call(
-        total_kernel, (like((chunk, LANES)),) + (like((cube, feat_tall, LANES)),) * cubes, micros=1
+    total, feat = call(
+        total_kernel, (like((chunk, LANES)), like((cube, cubes * feat_tall, LANES))), micros=1
     )(exchange(joined, cube))
     stride = cube
     while 2 * stride < space:
         total = (total.astype(F32) + from_partner(total, stride).astype(F32)).astype(BF16)
         stride *= 2
-    other = from_partner(total, stride) if stride < space else jnp.zeros_like(total)
-    copies = call(pair_kernel, like((cube, chunk, LANES)), micros=1)(total, other)
-    mine = exchange(copies, cube)
-    feats[1:] = [from_partner(feats[change], change * cube) for change in range(1, cubes)]
-    mine, feats = lax.optimization_barrier((mine, feats))
-    came = swapped(mine)
     features = call(
-        functools.partial(features_kernel, feat_rows),
+        functools.partial(features_kernel, feat_rows, cubes),
         like((out_chan, space, cells // space)),
         [pltpu.VMEM((space * feat_tall, LANES), F32)],
         micros=1,
-    )(*feats)
+    )(feat)
+    other = from_partner(total, stride) if stride < space else jnp.zeros_like(total)
+    other, features = lax.optimization_barrier((other, features))
+    copies = call(pair_kernel, like((cube, chunk, LANES)), micros=1)(total, other)
+    mine = exchange(copies, cube)
+    came = swapped(mine)
     anywhere = pl.BlockSpec(memory_space=pl.ANY)
     begun = call(
         functools.partial(own_half_kernel, places, panels, middle, 1.0 / total_two),

time: 66.1 us -> 65.2 us (0.986)
  blocking collectives: 17.1 us -> 24 us
  waiting for transfers between devices: 11.3 us -> 6.27 us
  starting transfers between devices: 14.4 us -> 12.9 us
  Pallas kernels: 15.9 us -> 14.7 us
    all_to_all x1 -> x2, blocking collectives: 17.1 us -> 24 us  [exchange(): lax.all_to_all(parts, 'space', split_axis=0, concat_axis=0, axis_index_gr...]
    all_to_all x1 -> x0, starting transfers between devices: 3.48 us -> none  [exchange(): lax.all_to_all(parts, 'space', split_axis=0, concat_axis=0, axis_index_gr...]
    all_to_all x1 -> x0, waiting for transfers between devices: 2.57 us -> none  [exchange(): lax.all_to_all(parts, 'space', split_axis=0, concat_axis=0, axis_index_gr...]
    ppermute x2, starting transfers between devices: 4.65 us -> 6.69 us  [from_partner(): lax.ppermute(block, 'space', [(i, i ^ stride) for i in range(lax.axis_siz...]
    ppermute x2, waiting for transfers between devices: 1.56 us -> 0.01 us  [passed_along(): return lax.ppermute(block, axis, route)]
    ppermute x2, waiting for transfers between devices: 7.13 us -> 5.84 us  [from_partner(): lax.ppermute(block, 'space', [(i, i ^ stride) for i in range(lax.axis_siz...]
    pallas_call x1, Pallas kernels: 0.81 us -> 0.04 us  [local(): call(pair_kernel, like((cube, chunk, LANES)), micros=1)(total, other)]
  transfers between devices with their start and end apart: 7 -> 6, of which waited for: 4 -> 3; matrix products, arithmetic and copies ran while one was open for 0% -> 0% of each run, Pallas kernels for 16% -> 16%
where the time goes in v1:
time: 65.2 us; the launch traced here: 64.7 us
  blocking collectives  24 us (37%)
  Pallas kernels  14.7 us (23%)
  starting transfers between devices  12.9 us (20%)
  waiting for transfers between devices  6.27 us (10%)
  local copies, waits for them, and re-layouts  6.06 us (9%)
  between operations  0.78 us (1%)
    all_to_all x2, blocking collectives, exchange(): lax.all_to_all(parts, 'space', split_axis=0, concat_axis=0, axis_index_gr...  24 us
    ppermute x2, starting transfers between devices, from_partner(): lax.ppermute(block, 'space', [(i, i ^ stride) for i in range(lax.axis_siz...  6.69 us
    ppermute x2, starting transfers between devices, passed_along(): return lax.ppermute(block, axis, route)  6.16 us
    ppermute x2, waiting for transfers between devices, from_partner(): lax.ppermute(block, 'space', [(i, i ^ stride) for i in range(lax.axis_siz...  5.84 us
    unnamed x20, local copies, waits for them, and re-layouts  5.03 us
    pallas_call x1, Pallas kernels, local(): call(own_kernel, (like((tall, cells), F32), like((tall, cells), F32), lik...  3.17 us
    pallas_call x1, Pallas kernels, local(): call(functools.partial(forward_kernel, 1.0 / math.sqrt(total_two)), (like...  2.56 us
    pallas_call x1, Pallas kernels, local(): call(functools.partial(sums_kernel, places, rows_two), (like((half, LANES...  2.17 us
  transfers between devices with their start and end apart: 6, of which 3 were waited for; matrix products, arithmetic and copies ran while one was open for 0% of the time, Pallas kernels for 16%

profile of v1, /device:TPU:0, one launch (start us, length us, event | category | flops | bytes accessed | tf_op | source)
XLA Modules:
  0.0 64.7 jit_solution(12581369136351104154)
XLA Ops:
  0.6 1.0 %slice.8 = bf16[4,3,128,128]{3,2,1,0:T(8,128)(2,1)S(1)} slice(bf16[4,4,128,128]{3,2,1,0:T(8,128)(2,1)} %bitcast.9), slice={[0:4], [1:4], [0:128], [0:128]} | slice | bytes 786432 | tf_op jit(solution)/shard_map/slice | solution.py:703
  1.7 4.9 %collective-permute-start = (bf16[4,3,128,128]{3,2,1,0:T(8,128)(2,1)S(1)}, bf16[4,3,128,128]{3,2,1,0:T(8,128)(2,1)S(1)}, u32[]{:S(2)}, u32[]{:S(2)}) collective-permute-start(bf16[4,3,128,128]{3,2,1,0:T(8,128)(2,1)S(1)} %slice.8), channel_id=1, source_target_pairs={{0,2},{2,4},{4,6},{6,8},{8,10},{10,12},{12,14},{14,16},{16,18},{18... | collective-permute-start | bytes 1179656 | tf_op jit(solution)/shard_map/ppermute | solution.py:667
  6.5 0.0 copy-start.3
  6.6 0.9 %copy-done.3 = bf16[864,64]{0,1:T(8,128)(2,1)S(1)} copy-done((bf16[864,64]{0,1:T(8,128)(2,1)S(1)}, bf16[864,64]{0,1:T(8,128)(2,1)}, u32[]{:S(2)}) %copy-start.3) | copy-done | bytes 110616
  7.4 0.7 %copy-done.5 = bf16[108,32]{0,1:T(8,128)(2,1)S(1)} copy-done((bf16[108,32]{0,1:T(8,128)(2,1)S(1)}, bf16[108,32]{0,1:T(8,128)(2,1)}, u32[]{:S(2)}) %copy-start.5) | copy-done | bytes 6936
  8.1 1.2 %copy-done.6 = bf16[8,112,400]{2,1,0:T(8,128)(2,1)S(1)} copy-done((bf16[8,112,400]{2,1,0:T(8,128)(2,1)S(1)}, bf16[8,112,400]{2,1,0:T(8,128)(2,1)}, u32[]{:S(2)}) %copy-start.6) | copy-done | bytes 716824
  9.3 1.1 %copy-done.8 = bf16[8,112,304]{2,1,0:T(8,128)(2,1)S(1)} copy-done((bf16[8,112,304]{2,1,0:T(8,128)(2,1)S(1)}, bf16[8,112,304]{2,1,0:T(8,128)(2,1)}, u32[]{:S(2)}) %copy-start.8) | copy-done | bytes 544792
  10.4 0.4 shard_map.126
  10.8 0.7 %copy-done.1 = bf16[4,1,4,128,128]{4,3,2,1,0:T(8,128)(2,1)S(1)} copy-done((bf16[4,1,4,128,128]{4,3,2,1,0:T(8,128)(2,1)S(1)}, bf16[4,1,4,128,128]{4,3,2,1,0:T(8,128)(2,1)}, u32[]{:S(2)}) %copy-start.1) | copy-done | bytes 524312
  11.5 0.3 copy-done.7
  11.8 0.2 copy-done.9
  11.9 3.2 %shard_map.127 = (f32[128,1024]{1,0:T(8,128)S(1)}, f32[128,1024]{1,0:T(8,128)S(1)}, f32[128,1024]{1,0:T(8,128)S(1)}, bf16[8,112,1024]{2,1,0:T(8,128)(2,1)S(1)}, f32[112,112]{1,0:T(8,128)S(1)}) custom-call(bf16[4,4,128,128]{3,2,1,0:T(8,128)(2,1)S(1)} %bitcast.10, bf16[256,400]{1,0:T(8,128)(2,1)S(1)} %get-tuple-element.41.wide_ref, ...), custom_call_target="tpu_custom_call" | custom-call | flops 6600000000 | bytes 1048576 | tf_op jit(solution)/shard_map/pallas_call | solution.py:713
  15.2 0.0 copy-start
  15.2 2.6 %shard_map.128 = (bf16[64,1024]{1,0:T(8,128)(2,1)S(1)}, bf16[896,1024]{1,0:T(8,128)(2,1)S(1)}, f32[128,1024]{1,0:T(8,128)S(1)}, bf16[304,1024]{1,0:T(8,128)(2,1)...) custom-call(bf16[4,3,128,128]{3,2,1,0:T(8,128)(2,1)S(1)} %collective-permute-done.halo_ref, ...), custom_call_target="tpu_custom_call" | custom-call | flops 5500000256 | bytes 1048576 | tf_op jit(solution)/shard_map/pallas_call | solution.py:730
  17.7 1.3 %collective-permute-start.3 = (bf16[64,1024]{1,0:T(8,128)(2,1)S(1)}, bf16[64,1024]{1,0:T(8,128)(2,1)S(1)}, u32[]{:S(2)}, u32[]{:S(2)}) collective-permute-start(bf16[64,1024]{1,0:T(8,128)(2,1)S(1)} %get-tuple-element.45.grad_ref), channel_id=1, source_target_pairs={{2,0},{4,2},{6,4},{8,6},{10,8},{12,10},{14,12},{16,14},{18,16},{20... | collective-permute-start | bytes 393224 | tf_op jit(solution)/shard_map/ppermute | solution.py:667
  19.0 6.3 %collective-permute-start.2 = (bf16[8,32,128]{2,1,0:T(8,128)(2,1)S(1)}, bf16[8,32,128]{2,1,0:T(8,128)(2,1)S(1)}, u32[]{:S(2)}, u32[]{:S(2)}) collective-permute-start(bf16[8,32,128]{2,1,0:T(8,128)(2,1)S(1)} %get-tuple-element.49), channel_id=1, source_target_pairs={{0,16},{2,18},{4,20},{6,22},{8,24},{10,26},{12,28},{14,30},{16,0},... | collective-permute-start | bytes 196616 | tf_op jit(solution)/shard_map/ppermute | solution.py:650
  25.3 2.2 %shard_map.129 = (bf16[1792,128]{1,0:T(8,128)(2,1)S(1)}, bf16[1792,128]{1,0:T(8,128)(2,1)S(1)}, f32[8,128]{1,0:T(8,128)S(1)}) custom-call(bf16[896,1024]{1,0:T(8,128)(2,1)S(1)} %get-tuple-element.44.p2_ref, bf16[64,1024]{1,0:T(8,128)(2,1)S(1)} %get-tuple-element.45.grad_ref), custom_call_target="tpu_custom_call" | custom-call | flops 110000000 | bytes 1048576 | tf_op jit(solution)/shard_map/pallas_call | solution.py:750
  27.5 0.1 collective-permute-start.1
  27.6 1.5 %shard_map.130 = (f32[112,112]{1,0:T(8,128)S(1)}, f32[32,144]{1,0:T(8,128)S(1)}, f32[128,1024]{1,0:T(8,128)S(1)}) custom-call(bf16[64,1024]{1,0:T(8,128)(2,1)S(1)} %get-tuple-element.45.grad_ref, bf16[256,512]{1,0:T(8,128)(2,1)S(1)} %get-tuple-element.51.back_ref, f32[128,1024]{1,0:T(8,128)S(1)} %get-tuple-element.52.slope_ref, ...), custom_call_target="tpu_custom_call" | custom-call | flops 110000000 | bytes 1048576 | tf_op jit(solution)/shard_map/pallas_call | solution.py:757
  29.1 1.3 %collective-permute-done.2.refs_1_ = bf16[8,32,128]{2,1,0:T(8,128)(2,1)S(1)} collective-permute-done((bf16[8,32,128]{2,1,0:T(8,128)(2,1)S(1)}, bf16[8,32,128]{2,1,0:T(8,128)(2,1)S(1)}, u32[]{:S(2)}, u32[]{:S(2)}) %collective-permute-start.2) | collective-permute-done | bytes 65568 | tf_op jit(solution)/shard_map/ppermute | solution.py:650
  30.4 0.7 %shard_map.131.small_ref = bf16[128,128]{1,0:T(8,128)(2,1)S(1)} custom-call(bf16[64,1024]{1,0:T(8,128)(2,1)S(1)} %collective-permute-done.3.above_ref, bf16[256,512]{1,0:T(8,128)(2,1)S(1)} %get-tuple-element.51.back_ref, f32[128,1024]{1,0:T(8,128)S(1)} %get-tuple-element.57.high_ref, f32[128,1024]{1,0:T(8,128)S(1)} %get-tuple-element.58.slope_ref, ...), custom_call_target="tpu_custom_call" | custom-call | flops 13200000000 | bytes 1048576 | tf_op jit(solution)/shard_map/pallas_call | solution.py:763
  31.2 0.0 collective-permute-done.1.came_ref
  31.2 0.1 shard_map.132
  31.3 13.7 %all_to_all.10.came_ref = bf16[8,304,128]{2,1,0:T(8,128)(2,1)S(1)} all-to-all(bf16[8,304,128]{2,1,0:T(8,128)(2,1)S(1)} %shard_map.132), channel_id=1, replica_groups={{0,2,4,6,8,10,12,14},{16,18,20,22,24,26,28,30},{1,3,5,7,9,11,13,15},{17..., dimensions={0} | all-to-all | bytes 1245184 | tf_op jit(solution)/shard_map/all_to_all | solution.py:646
  44.9 0.1 shard_map.133
  45.0 0.4 collective-permute-start.4
  45.4 1.0 %shard_map.134 = bf16[64,16,64]{2,1,0:T(8,128)(2,1)} custom-call(bf16[8,64,128]{2,1,0:T(8,128)(2,1)S(1)} %get-tuple-element.64.feat_ref), custom_call_target="tpu_custom_call" | custom-call | flops 1100000000 | bytes 1048576 | tf_op jit(solution)/shard_map/pallas_call | solution.py:777
  46.4 4.5 %collective-permute-done.4.came_ref = bf16[240,128]{1,0:T(8,128)(2,1)S(1)} collective-permute-done((bf16[240,128]{1,0:T(8,128)(2,1)S(1)}, bf16[240,128]{1,0:T(8,128)(2,1)S(1)}, u32[]{:S(2)}, u32[]{:S(2)}) %collective-permute-start.4) | collective-permute-done | bytes 61472 | tf_op jit(solution)/shard_map/ppermute | solution.py:650
  50.9 10.3 %all_to_all.11.mine_ref = bf16[8,240,128]{2,1,0:T(8,128)(2,1)S(1)} all-to-all(bf16[8,240,128]{2,1,0:T(8,128)(2,1)S(1)} %shard_map.135), channel_id=1, replica_groups={{0,2,4,6,8,10,12,14},{16,18,20,22,24,26,28,30},{1,3,5,7,9,11,13,15},{17..., dimensions={0} | all-to-all | bytes 983040 | tf_op jit(solution)/shard_map/all_to_all | solution.py:646
  61.2 1.4 %shard_map.136.begun_ref = f32[864,864]{1,0:T(8,128)} custom-call(bf16[8,240,128]{2,1,0:T(8,128)(2,1)S(1)} %all_to_all.11.mine_ref), custom_call_target="tpu_custom_call" | custom-call | flops 2200000000 | bytes 1048576 | tf_op jit(solution)/shard_map/pallas_call | solution.py:789
  62.6 0.4 collective-permute-done.5.came_ref
  63.1 1.7 %shard_map.137 = (f32[108,108]{1,0:T(8,128)}, f32[864,864]{1,0:T(8,128)}, f32[32,32]{1,0:T(8,128)}, f32[64,64]{1,0:T(8,128)}, f32[32,108]{1,0:T(8,128)}, /*index=5*/f32[64,864]{1,0:T(8,128)}) custom-call(f32[864,864]{1,0:T(8,128)} %shard_map.136.begun_ref, bf16[8,240,128]{2,1,0:T(8,128)(2,1)S(1)} %all_to_all.11.mine_ref, ...), custom_call_target="tpu_custom_call", output_to_operand_aliasing={{1}: (0, {})} | custom-call | flops 2200000000 | bytes 1048576 | tf_op jit(solution)/shard_map/pallas_call | solution.py:811
  (15 shorter events, 0.1 us)
Async XLA Ops:
  1.7 13.5 %collective-permute-start = (bf16[4,3,128,128]{3,2,1,0:T(8,128)(2,1)S(1)}, bf16[4,3,128,128]{3,2,1,0:T(8,128)(2,1)S(1)}, u32[]{:S(2)}, u32[]{:S(2)}) collective-permute-start(bf16[4,3,128,128]{3,2,1,0:T(8,128)(2,1)S(1)} %slice.8), channel_id=1, source_target_pairs={{0,2},{2,4},{4,6},{6,8},{8,10},{10,12},{12,14},{14,16},{16,18},{18... | collective-permute-start | bytes 1179656 | tf_op jit(solution)/shard_map/ppermute | solution.py:667
  6.5 0.9 %copy-start.3 = (bf16[864,64]{0,1:T(8,128)(2,1)S(1)}, bf16[864,64]{0,1:T(8,128)(2,1)}, u32[]{:S(2)}) copy-start(bf16[864,64]{0,1:T(8,128)(2,1)} %param.9) | copy-start | bytes 331780
  7.4 0.7 %copy-start.5 = (bf16[108,32]{0,1:T(8,128)(2,1)S(1)}, bf16[108,32]{0,1:T(8,128)(2,1)}, u32[]{:S(2)}) copy-start(bf16[108,32]{0,1:T(8,128)(2,1)} %param.8) | copy-start | bytes 20740
  8.1 1.2 %copy-start.6 = (bf16[8,112,400]{2,1,0:T(8,128)(2,1)S(1)}, bf16[8,112,400]{2,1,0:T(8,128)(2,1)}, u32[]{:S(2)}) copy-start(bf16[8,112,400]{2,1,0:T(8,128)(2,1)} %constant.7.clone.own_rows_ref.rows_ref) | copy-start | bytes 2150404
  9.3 1.1 %copy-start.8 = (bf16[8,112,304]{2,1,0:T(8,128)(2,1)S(1)}, bf16[8,112,304]{2,1,0:T(8,128)(2,1)}, u32[]{:S(2)}) copy-start(bf16[8,112,304]{2,1,0:T(8,128)(2,1)} %constant.6.clone.halo_rows_ref) | copy-start | bytes 1634308
  10.4 1.0 %copy-start.1 = (bf16[4,1,4,128,128]{4,3,2,1,0:T(8,128)(2,1)S(1)}, bf16[4,1,4,128,128]{4,3,2,1,0:T(8,128)(2,1)}, u32[]{:S(2)}) copy-start(bf16[4,1,4,128,128]{4,3,2,1,0:T(8,128)(2,1)} %param.7) | copy-start | bytes 1572868
  10.4 1.3 %copy-start.7 = (bf16[8,112,400]{2,1,0:T(8,128)(2,1)S(1)}, bf16[8,112,400]{2,1,0:T(8,128)(2,1)}, u32[]{:S(2)}) copy-start(bf16[8,112,400]{2,1,0:T(8,128)(2,1)} %constant.7.clone.own_rows_ref.rows_ref) | copy-start | bytes 2150404
  10.4 1.5 %copy-start.9 = (bf16[512,640]{1,0:T(8,128)(2,1)S(1)}, bf16[512,640]{1,0:T(8,128)(2,1)}, u32[]{:S(2)}) copy-start(bf16[512,640]{1,0:T(8,128)(2,1)} %constant.8.clone.split_ref) | copy-start | bytes 1966084
  11.9 3.2 %copy-start.2 = (bf16[64,1,1,1024]{3,0,2,1:T(8,128)(2,1)S(1)}, bf16[64,1,1,1024]{3,0,2,1:T(8,128)(2,1)}, u32[]{:S(2)}) copy-start(bf16[64,1,1,1024]{3,0,2,1:T(8,128)(2,1)} %param.10) | copy-start | bytes 393220
  11.9 3.2 %copy-start.4 = (bf16[864,64]{0,1:T(8,128)(2,1)S(1)}, bf16[864,64]{0,1:T(8,128)(2,1)}, u32[]{:S(2)}) copy-start(bf16[864,64]{0,1:T(8,128)(2,1)} %param.9) | copy-start | bytes 331780
  15.2 12.4 %copy-start = (bf16[4,112,304]{2,1,0:T(8,128)(2,1)S(1)}, bf16[4,112,304]{2,1,0:T(8,128)(2,1)}, u32[]{:S(2)}) copy-start(bf16[4,112,304]{2,1,0:T(8,128)(2,1)} %constant.11.rows_ref) | copy-start | bytes 817156
  17.7 12.7 %collective-permute-start.3 = (bf16[64,1024]{1,0:T(8,128)(2,1)S(1)}, bf16[64,1024]{1,0:T(8,128)(2,1)S(1)}, u32[]{:S(2)}, u32[]{:S(2)}) collective-permute-start(bf16[64,1024]{1,0:T(8,128)(2,1)S(1)} %get-tuple-element.45.grad_ref), channel_id=1, source_target_pairs={{2,0},{4,2},{6,4},{8,6},{10,8},{12,10},{14,12},{16,14},{18,16},{20... | collective-permute-start | bytes 393224 | tf_op jit(solution)/shard_map/ppermute | solution.py:667
  19.0 11.4 %collective-permute-start.2 = (bf16[8,32,128]{2,1,0:T(8,128)(2,1)S(1)}, bf16[8,32,128]{2,1,0:T(8,128)(2,1)S(1)}, u32[]{:S(2)}, u32[]{:S(2)}) collective-permute-start(bf16[8,32,128]{2,1,0:T(8,128)(2,1)S(1)} %get-tuple-element.49), channel_id=1, source_target_pairs={{0,16},{2,18},{4,20},{6,22},{8,24},{10,26},{12,28},{14,30},{16,0},... | collective-permute-start | bytes 196616 | tf_op jit(solution)/shard_map/ppermute | solution.py:650
  27.5 3.6 %collective-permute-start.1 = (bf16[1792,128]{1,0:T(8,128)(2,1)S(1)}, bf16[1792,128]{1,0:T(8,128)(2,1)S(1)}, u32[]{:S(2)}, u32[]{:S(2)}) collective-permute-start(bf16[1792,128]{1,0:T(8,128)(2,1)S(1)} %get-tuple-element.47), channel_id=1, source_target_pairs={{0,1},{1,0},{2,3},{3,2},{4,5},{5,4},{6,7},{7,6},{8,9},{9,8},{10,11... | collective-permute-start | bytes 1376264 | tf_op jit(solution)/shard_map/ppermute | solution.py:671
  45.0 5.8 %collective-permute-start.4 = (bf16[240,128]{1,0:T(8,128)(2,1)S(1)}, bf16[240,128]{1,0:T(8,128)(2,1)S(1)}, u32[]{:S(2)}, u32[]{:S(2)}) collective-permute-start(bf16[240,128]{1,0:T(8,128)(2,1)S(1)} %get-tuple-element.63.mine_ref), channel_id=1, source_target_pairs={{0,16},{2,18},{4,20},{6,22},{8,24},{10,26},{12,28},{14,30},{16,0},... | collective-permute-start | bytes 184328 | tf_op jit(solution)/shard_map/ppermute | solution.py:650
  61.2 1.9 %collective-permute-start.5 = (bf16[8,240,128]{2,1,0:T(8,128)(2,1)S(1)}, bf16[8,240,128]{2,1,0:T(8,128)(2,1)S(1)}, u32[]{:S(2)}, u32[]{:S(2)}) collective-permute-start(bf16[8,240,128]{2,1,0:T(8,128)(2,1)S(1)} %all_to_all.11.mine_ref), channel_id=1, source_target_pairs={{0,1},{1,0},{2,3},{3,2},{4,5},{5,4},{6,7},{7,6},{8,9},{9,8},{10,11... | collective-permute-start | bytes 1474568 | tf_op jit(solution)/shard_map/ppermute | solution.py:671

commit v2 on v1

--- a/solution.py
+++ b/solution.py
@@ -454,7 +454,7 @@
         out_ref[owner, large : large + small, :] = small_ref[owner * small : (owner + 1) * small, :]
         for change, feat_ref in enumerate(feat_refs):
             start = large + small + change * feat_rows
-            out_ref[owner, start : start + feat_rows, :] = feat_ref[owner]
+            out_ref[owner, start : start + feat_rows, :] = feat_ref[walk(owners)[owner]]
 
 
 def total_kernel(came_ref, out_ref, feat_ref):
@@ -480,7 +480,7 @@
     cube = lax.axis_index("space") // members
     for change in range(cubes):
         for member in range(members):
-            start = pl.multiple_of(((cube ^ change) * members + member) * rows, 16)
+            start = pl.multiple_of(((cube ^ change) * members + walk(members)[member]) * rows, 16)
             scr[pl.ds(start, rows), :] = feat_ref[member, change * rows : (change + 1) * rows, :].astype(F32)
     for i in range(owned_rows):
         block = scr[pl.ds(i, owners, stride=rows), :]
@@ -640,9 +640,13 @@
     return 8 if space % 8 == 0 else space
 
 
+def walk(size):
+    return [at ^ (at >> 1) for at in range(size)]
+
+
 def exchange(parts, size):
     space = lax.axis_size("space")
-    groups = [list(range(base, base + size)) for base in range(0, space, size)]
+    groups = [[base + at for at in walk(size)] for base in range(0, space, size)]
     return lax.all_to_all(parts, "space", split_axis=0, concat_axis=0, axis_index_groups=groups)
 
 
@@ -677,9 +681,9 @@
 
 def split_scratch(count, plane):
     return [
-        pltpu.VMEM((count * (plane + 8), plane), F32),
+        pltpu.VMEM((count * (plane + 8) + 16, plane), F32),
         pltpu.VMEM((count * 40, 4 * plane), BF16),
-        pltpu.VMEM((8 * up_to(25 * count, 16), LANES), F32),
+        pltpu.VMEM((8 * up_to(25 * count, 16) + 8, LANES), F32),
     ]
 
 
@@ -707,7 +711,7 @@
     halo_wide, own_wide, back = call(
         prepare_kernel,
         (like((2 * tall, halo_width)), like((2 * tall, own_width)), like((2 * tall, 8 * out_chan))),
-        [pltpu.VMEM((rows_two, LANES), F32)],
+        [pltpu.VMEM((rows_two + 32, LANES), F32)],
         micros=3,
     )(kernel_one.T, kernel_two.T, halo_rows, own_rows)
     part, act_high, slope_high, p1, in_one_part = call(
@@ -737,7 +741,7 @@
         )
         + (like((cube, feat_tall, LANES)),) * cubes,
         split_scratch(channels * halo, plane)
-        + [pltpu.VMEM((rows_two * (cells // LANES), LANES), F32), pltpu.VMEM((space, feat_tall, LANES), BF16)],
+        + [pltpu.VMEM((rows_two * (cells // LANES) + 32, LANES), F32), pltpu.VMEM((space, feat_tall, LANES), BF16)],
         micros=5,
     )(halo_block, halo_wide, split, part, act_high, kernel_two.T, cotangent.reshape(out_chan, cells))
     feats = feats[:1] + [from_partner(feats[change], change * cube) for change in range(1, cubes)]
@@ -777,7 +781,7 @@
     features = call(
         functools.partial(features_kernel, feat_rows, cubes),
         like((out_chan, space, cells // space)),
-        [pltpu.VMEM((space * feat_tall, LANES), F32)],
+        [pltpu.VMEM(((space + 1) * feat_tall, LANES), F32)],
         micros=1,
     )(feat)
     other = from_partner(total, stride) if stride < space else jnp.zeros_like(total)

time: 65.2 us -> 64.6 us (level)
  no operation moved by 1% of the time
where the time goes in v2:
time: 64.6 us; the launch traced here: 64.1 us
  blocking collectives  23.4 us (36%)
  Pallas kernels  14.7 us (23%)
  starting transfers between devices  12.9 us (20%)
  waiting for transfers between devices  6.25 us (10%)
  local copies, waits for them, and re-layouts  6.06 us (9%)
  between operations  0.78 us (1%)
    all_to_all x2, blocking collectives, exchange(): lax.all_to_all(parts, 'space', split_axis=0, concat_axis=0, axis_index_gr...  23.4 us
    ppermute x2, starting transfers between devices, from_partner(): lax.ppermute(block, 'space', [(i, i ^ stride) for i in range(lax.axis_siz...  6.69 us
    ppermute x2, starting transfers between devices, passed_along(): return lax.ppermute(block, axis, route)  6.16 us
    ppermute x2, waiting for transfers between devices, from_partner(): lax.ppermute(block, 'space', [(i, i ^ stride) for i in range(lax.axis_siz...  5.82 us
    unnamed x20, local copies, waits for them, and re-layouts  5.03 us
    pallas_call x1, Pallas kernels, local(): call(own_kernel, (like((tall, cells), F32), like((tall, cells), F32), lik...  3.18 us
    pallas_call x1, Pallas kernels, local(): call(functools.partial(forward_kernel, 1.0 / math.sqrt(total_two)), (like...  2.57 us
    pallas_call x1, Pallas kernels, local(): call(functools.partial(sums_kernel, places, rows_two), (like((half, LANES...  2.17 us
  transfers between devices with their start and end apart: 6, of which 3 were waited for; matrix products, arithmetic and copies ran while one was open for 0% of the time, Pallas kernels for 16%

profile of v2, /device:TPU:0, one launch (start us, length us, event | category | flops | bytes accessed | tf_op | source)
XLA Modules:
  0.0 64.1 jit_solution(5537536126169312398)
XLA Ops:
  0.6 1.0 %slice.8 = bf16[4,3,128,128]{3,2,1,0:T(8,128)(2,1)S(1)} slice(bf16[4,4,128,128]{3,2,1,0:T(8,128)(2,1)} %bitcast.9), slice={[0:4], [1:4], [0:128], [0:128]} | slice | bytes 786432 | tf_op jit(solution)/shard_map/slice | solution.py:707
  1.7 4.9 %collective-permute-start = (bf16[4,3,128,128]{3,2,1,0:T(8,128)(2,1)S(1)}, bf16[4,3,128,128]{3,2,1,0:T(8,128)(2,1)S(1)}, u32[]{:S(2)}, u32[]{:S(2)}) collective-permute-start(bf16[4,3,128,128]{3,2,1,0:T(8,128)(2,1)S(1)} %slice.8), channel_id=1, source_target_pairs={{0,2},{2,4},{4,6},{6,8},{8,10},{10,12},{12,14},{14,16},{16,18},{18... | collective-permute-start | bytes 1179656 | tf_op jit(solution)/shard_map/ppermute | solution.py:671
  6.5 0.0 copy-start.3
  6.6 0.9 %copy-done.3 = bf16[864,64]{0,1:T(8,128)(2,1)S(1)} copy-done((bf16[864,64]{0,1:T(8,128)(2,1)S(1)}, bf16[864,64]{0,1:T(8,128)(2,1)}, u32[]{:S(2)}) %copy-start.3) | copy-done | bytes 110616
  7.4 0.7 %copy-done.5 = bf16[108,32]{0,1:T(8,128)(2,1)S(1)} copy-done((bf16[108,32]{0,1:T(8,128)(2,1)S(1)}, bf16[108,32]{0,1:T(8,128)(2,1)}, u32[]{:S(2)}) %copy-start.5) | copy-done | bytes 6936
  8.1 1.2 %copy-done.6 = bf16[8,112,400]{2,1,0:T(8,128)(2,1)S(1)} copy-done((bf16[8,112,400]{2,1,0:T(8,128)(2,1)S(1)}, bf16[8,112,400]{2,1,0:T(8,128)(2,1)}, u32[]{:S(2)}) %copy-start.6) | copy-done | bytes 716824
  9.3 1.1 %copy-done.8 = bf16[8,112,304]{2,1,0:T(8,128)(2,1)S(1)} copy-done((bf16[8,112,304]{2,1,0:T(8,128)(2,1)S(1)}, bf16[8,112,304]{2,1,0:T(8,128)(2,1)}, u32[]{:S(2)}) %copy-start.8) | copy-done | bytes 544792
  10.4 0.4 shard_map.126
  10.8 0.7 %copy-done.1 = bf16[4,1,4,128,128]{4,3,2,1,0:T(8,128)(2,1)S(1)} copy-done((bf16[4,1,4,128,128]{4,3,2,1,0:T(8,128)(2,1)S(1)}, bf16[4,1,4,128,128]{4,3,2,1,0:T(8,128)(2,1)}, u32[]{:S(2)}) %copy-start.1) | copy-done | bytes 524312
  11.5 0.3 copy-done.7
  11.8 0.2 copy-done.9
  11.9 3.2 %shard_map.127 = (f32[128,1024]{1,0:T(8,128)S(1)}, f32[128,1024]{1,0:T(8,128)S(1)}, f32[128,1024]{1,0:T(8,128)S(1)}, bf16[8,112,1024]{2,1,0:T(8,128)(2,1)S(1)}, f32[112,112]{1,0:T(8,128)S(1)}) custom-call(bf16[4,4,128,128]{3,2,1,0:T(8,128)(2,1)S(1)} %bitcast.10, bf16[256,400]{1,0:T(8,128)(2,1)S(1)} %get-tuple-element.41.wide_ref, ...), custom_call_target="tpu_custom_call" | custom-call | flops 6600000000 | bytes 1048576 | tf_op jit(solution)/shard_map/pallas_call | solution.py:717
  15.1 0.0 collective-permute-done.halo_ref
  15.2 0.0 copy-start
  15.2 2.6 %shard_map.128 = (bf16[64,1024]{1,0:T(8,128)(2,1)S(1)}, bf16[896,1024]{1,0:T(8,128)(2,1)S(1)}, f32[128,1024]{1,0:T(8,128)S(1)}, bf16[304,1024]{1,0:T(8,128)(2,1)...) custom-call(bf16[4,3,128,128]{3,2,1,0:T(8,128)(2,1)S(1)} %collective-permute-done.halo_ref, ...), custom_call_target="tpu_custom_call" | custom-call | flops 5500000256 | bytes 1048576 | tf_op jit(solution)/shard_map/pallas_call | solution.py:734
  17.8 1.3 %collective-permute-start.3 = (bf16[64,1024]{1,0:T(8,128)(2,1)S(1)}, bf16[64,1024]{1,0:T(8,128)(2,1)S(1)}, u32[]{:S(2)}, u32[]{:S(2)}) collective-permute-start(bf16[64,1024]{1,0:T(8,128)(2,1)S(1)} %get-tuple-element.45.grad_ref), channel_id=1, source_target_pairs={{2,0},{4,2},{6,4},{8,6},{10,8},{12,10},{14,12},{16,14},{18,16},{20... | collective-permute-start | bytes 393224 | tf_op jit(solution)/shard_map/ppermute | solution.py:671
  19.1 6.3 %collective-permute-start.2 = (bf16[8,32,128]{2,1,0:T(8,128)(2,1)S(1)}, bf16[8,32,128]{2,1,0:T(8,128)(2,1)S(1)}, u32[]{:S(2)}, u32[]{:S(2)}) collective-permute-start(bf16[8,32,128]{2,1,0:T(8,128)(2,1)S(1)} %get-tuple-element.49), channel_id=1, source_target_pairs={{0,16},{2,18},{4,20},{6,22},{8,24},{10,26},{12,28},{14,30},{16,0},... | collective-permute-start | bytes 196616 | tf_op jit(solution)/shard_map/ppermute | solution.py:654
  25.3 2.2 %shard_map.129 = (bf16[1792,128]{1,0:T(8,128)(2,1)S(1)}, bf16[1792,128]{1,0:T(8,128)(2,1)S(1)}, f32[8,128]{1,0:T(8,128)S(1)}) custom-call(bf16[896,1024]{1,0:T(8,128)(2,1)S(1)} %get-tuple-element.44.p2_ref, bf16[64,1024]{1,0:T(8,128)(2,1)S(1)} %get-tuple-element.45.grad_ref), custom_call_target="tpu_custom_call" | custom-call | flops 110000000 | bytes 1048576 | tf_op jit(solution)/shard_map/pallas_call | solution.py:754
  27.5 0.1 collective-permute-start.1
  27.6 1.5 %shard_map.130 = (f32[112,112]{1,0:T(8,128)S(1)}, f32[32,144]{1,0:T(8,128)S(1)}, f32[128,1024]{1,0:T(8,128)S(1)}) custom-call(bf16[64,1024]{1,0:T(8,128)(2,1)S(1)} %get-tuple-element.45.grad_ref, bf16[256,512]{1,0:T(8,128)(2,1)S(1)} %get-tuple-element.51.back_ref, f32[128,1024]{1,0:T(8,128)S(1)} %get-tuple-element.52.slope_ref, ...), custom_call_target="tpu_custom_call" | custom-call | flops 110000000 | bytes 1048576 | tf_op jit(solution)/shard_map/pallas_call | solution.py:761
  29.1 1.3 %collective-permute-done.2.refs_1_ = bf16[8,32,128]{2,1,0:T(8,128)(2,1)S(1)} collective-permute-done((bf16[8,32,128]{2,1,0:T(8,128)(2,1)S(1)}, bf16[8,32,128]{2,1,0:T(8,128)(2,1)S(1)}, u32[]{:S(2)}, u32[]{:S(2)}) %collective-permute-start.2) | collective-permute-done | bytes 65568 | tf_op jit(solution)/shard_map/ppermute | solution.py:654
  30.4 0.7 %shard_map.131.small_ref = bf16[128,128]{1,0:T(8,128)(2,1)S(1)} custom-call(bf16[64,1024]{1,0:T(8,128)(2,1)S(1)} %collective-permute-done.3.above_ref, bf16[256,512]{1,0:T(8,128)(2,1)S(1)} %get-tuple-element.51.back_ref, f32[128,1024]{1,0:T(8,128)S(1)} %get-tuple-element.57.high_ref, f32[128,1024]{1,0:T(8,128)S(1)} %get-tuple-element.58.slope_ref, ...), custom_call_target="tpu_custom_call" | custom-call | flops 13200000000 | bytes 1048576 | tf_op jit(solution)/shard_map/pallas_call | solution.py:767
  31.2 0.1 shard_map.132
  31.3 13.4 %all_to_all.10.came_ref = bf16[8,304,128]{2,1,0:T(8,128)(2,1)S(1)} all-to-all(bf16[8,304,128]{2,1,0:T(8,128)(2,1)S(1)} %shard_map.132), channel_id=1, replica_groups={{0,2,6,4,12,14,10,8},{16,18,22,20,28,30,26,24},{1,3,7,5,13,15,11,9},{17..., dimensions={0} | all-to-all | bytes 1245184 | tf_op jit(solution)/shard_map/all_to_all | solution.py:650
  44.7 0.1 shard_map.133
  44.8 0.4 collective-permute-start.4
  45.1 1.0 %shard_map.134 = bf16[64,16,64]{2,1,0:T(8,128)(2,1)} custom-call(bf16[8,64,128]{2,1,0:T(8,128)(2,1)S(1)} %get-tuple-element.64.feat_ref), custom_call_target="tpu_custom_call" | custom-call | flops 1100000000 | bytes 1048576 | tf_op jit(solution)/shard_map/pallas_call | solution.py:781
  46.1 4.5 %collective-permute-done.4.came_ref = bf16[240,128]{1,0:T(8,128)(2,1)S(1)} collective-permute-done((bf16[240,128]{1,0:T(8,128)(2,1)S(1)}, bf16[240,128]{1,0:T(8,128)(2,1)S(1)}, u32[]{:S(2)}, u32[]{:S(2)}) %collective-permute-start.4) | collective-permute-done | bytes 61472 | tf_op jit(solution)/shard_map/ppermute | solution.py:654
  50.6 10.0 %all_to_all.11.mine_ref = bf16[8,240,128]{2,1,0:T(8,128)(2,1)S(1)} all-to-all(bf16[8,240,128]{2,1,0:T(8,128)(2,1)S(1)} %shard_map.135), channel_id=1, replica_groups={{0,2,6,4,12,14,10,8},{16,18,22,20,28,30,26,24},{1,3,7,5,13,15,11,9},{17..., dimensions={0} | all-to-all | bytes 983040 | tf_op jit(solution)/shard_map/all_to_all | solution.py:650
  60.6 1.4 %shard_map.136.begun_ref = f32[864,864]{1,0:T(8,128)} custom-call(bf16[8,240,128]{2,1,0:T(8,128)(2,1)S(1)} %all_to_all.11.mine_ref), custom_call_target="tpu_custom_call" | custom-call | flops 2200000000 | bytes 1048576 | tf_op jit(solution)/shard_map/pallas_call | solution.py:793
  62.1 0.4 collective-permute-done.5.came_ref
  62.5 1.7 %shard_map.137 = (f32[108,108]{1,0:T(8,128)}, f32[864,864]{1,0:T(8,128)}, f32[32,32]{1,0:T(8,128)}, f32[64,64]{1,0:T(8,128)}, f32[32,108]{1,0:T(8,128)}, /*index=5*/f32[64,864]{1,0:T(8,128)}) custom-call(f32[864,864]{1,0:T(8,128)} %shard_map.136.begun_ref, bf16[8,240,128]{2,1,0:T(8,128)(2,1)S(1)} %all_to_all.11.mine_ref, ...), custom_call_target="tpu_custom_call", output_to_operand_aliasing={{1}: (0, {})} | custom-call | flops 2200000000 | bytes 1048576 | tf_op jit(solution)/shard_map/pallas_call | solution.py:815
  (15 shorter events, 0.1 us)
Async XLA Ops:
  1.7 13.5 %collective-permute-start = (bf16[4,3,128,128]{3,2,1,0:T(8,128)(2,1)S(1)}, bf16[4,3,128,128]{3,2,1,0:T(8,128)(2,1)S(1)}, u32[]{:S(2)}, u32[]{:S(2)}) collective-permute-start(bf16[4,3,128,128]{3,2,1,0:T(8,128)(2,1)S(1)} %slice.8), channel_id=1, source_target_pairs={{0,2},{2,4},{4,6},{6,8},{8,10},{10,12},{12,14},{14,16},{16,18},{18... | collective-permute-start | bytes 1179656 | tf_op jit(solution)/shard_map/ppermute | solution.py:671
  6.5 0.9 %copy-start.3 = (bf16[864,64]{0,1:T(8,128)(2,1)S(1)}, bf16[864,64]{0,1:T(8,128)(2,1)}, u32[]{:S(2)}) copy-start(bf16[864,64]{0,1:T(8,128)(2,1)} %param.9) | copy-start | bytes 331780
  7.4 0.7 %copy-start.5 = (bf16[108,32]{0,1:T(8,128)(2,1)S(1)}, bf16[108,32]{0,1:T(8,128)(2,1)}, u32[]{:S(2)}) copy-start(bf16[108,32]{0,1:T(8,128)(2,1)} %param.8) | copy-start | bytes 20740
  8.1 1.2 %copy-start.6 = (bf16[8,112,400]{2,1,0:T(8,128)(2,1)S(1)}, bf16[8,112,400]{2,1,0:T(8,128)(2,1)}, u32[]{:S(2)}) copy-start(bf16[8,112,400]{2,1,0:T(8,128)(2,1)} %constant.7.clone.own_rows_ref.rows_ref) | copy-start | bytes 2150404
  9.3 1.1 %copy-start.8 = (bf16[8,112,304]{2,1,0:T(8,128)(2,1)S(1)}, bf16[8,112,304]{2,1,0:T(8,128)(2,1)}, u32[]{:S(2)}) copy-start(bf16[8,112,304]{2,1,0:T(8,128)(2,1)} %constant.6.clone.halo_rows_ref) | copy-start | bytes 1634308
  10.4 1.0 %copy-start.1 = (bf16[4,1,4,128,128]{4,3,2,1,0:T(8,128)(2,1)S(1)}, bf16[4,1,4,128,128]{4,3,2,1,0:T(8,128)(2,1)}, u32[]{:S(2)}) copy-start(bf16[4,1,4,128,128]{4,3,2,1,0:T(8,128)(2,1)} %param.7) | copy-start | bytes 1572868
  10.4 1.3 %copy-start.7 = (bf16[8,112,400]{2,1,0:T(8,128)(2,1)S(1)}, bf16[8,112,400]{2,1,0:T(8,128)(2,1)}, u32[]{:S(2)}) copy-start(bf16[8,112,400]{2,1,0:T(8,128)(2,1)} %constant.7.clone.own_rows_ref.rows_ref) | copy-start | bytes 2150404
  10.4 1.5 %copy-start.9 = (bf16[512,640]{1,0:T(8,128)(2,1)S(1)}, bf16[512,640]{1,0:T(8,128)(2,1)}, u32[]{:S(2)}) copy-start(bf16[512,640]{1,0:T(8,128)(2,1)} %constant.8.clone.split_ref) | copy-start | bytes 1966084
  11.9 3.2 %copy-start.2 = (bf16[64,1,1,1024]{3,0,2,1:T(8,128)(2,1)S(1)}, bf16[64,1,1,1024]{3,0,2,1:T(8,128)(2,1)}, u32[]{:S(2)}) copy-start(bf16[64,1,1,1024]{3,0,2,1:T(8,128)(2,1)} %param.10) | copy-start | bytes 393220
  11.9 3.2 %copy-start.4 = (bf16[864,64]{0,1:T(8,128)(2,1)S(1)}, bf16[864,64]{0,1:T(8,128)(2,1)}, u32[]{:S(2)}) copy-start(bf16[864,64]{0,1:T(8,128)(2,1)} %param.9) | copy-start | bytes 331780
  15.2 12.4 %copy-start = (bf16[4,112,304]{2,1,0:T(8,128)(2,1)S(1)}, bf16[4,112,304]{2,1,0:T(8,128)(2,1)}, u32[]{:S(2)}) copy-start(bf16[4,112,304]{2,1,0:T(8,128)(2,1)} %constant.11.rows_ref) | copy-start | bytes 817156
  17.8 12.7 %collective-permute-start.3 = (bf16[64,1024]{1,0:T(8,128)(2,1)S(1)}, bf16[64,1024]{1,0:T(8,128)(2,1)S(1)}, u32[]{:S(2)}, u32[]{:S(2)}) collective-permute-start(bf16[64,1024]{1,0:T(8,128)(2,1)S(1)} %get-tuple-element.45.grad_ref), channel_id=1, source_target_pairs={{2,0},{4,2},{6,4},{8,6},{10,8},{12,10},{14,12},{16,14},{18,16},{20... | collective-permute-start | bytes 393224 | tf_op jit(solution)/shard_map/ppermute | solution.py:671
  19.1 11.4 %collective-permute-start.2 = (bf16[8,32,128]{2,1,0:T(8,128)(2,1)S(1)}, bf16[8,32,128]{2,1,0:T(8,128)(2,1)S(1)}, u32[]{:S(2)}, u32[]{:S(2)}) collective-permute-start(bf16[8,32,128]{2,1,0:T(8,128)(2,1)S(1)} %get-tuple-element.49), channel_id=1, source_target_pairs={{0,16},{2,18},{4,20},{6,22},{8,24},{10,26},{12,28},{14,30},{16,0},... | collective-permute-start | bytes 196616 | tf_op jit(solution)/shard_map/ppermute | solution.py:654
  27.5 3.6 %collective-permute-start.1 = (bf16[1792,128]{1,0:T(8,128)(2,1)S(1)}, bf16[1792,128]{1,0:T(8,128)(2,1)S(1)}, u32[]{:S(2)}, u32[]{:S(2)}) collective-permute-start(bf16[1792,128]{1,0:T(8,128)(2,1)S(1)} %get-tuple-element.47), channel_id=1, source_target_pairs={{0,1},{1,0},{2,3},{3,2},{4,5},{5,4},{6,7},{7,6},{8,9},{9,8},{10,11... | collective-permute-start | bytes 1376264 | tf_op jit(solution)/shard_map/ppermute | solution.py:675
  44.8 5.8 %collective-permute-start.4 = (bf16[240,128]{1,0:T(8,128)(2,1)S(1)}, bf16[240,128]{1,0:T(8,128)(2,1)S(1)}, u32[]{:S(2)}, u32[]{:S(2)}) collective-permute-start(bf16[240,128]{1,0:T(8,128)(2,1)S(1)} %get-tuple-element.63.mine_ref), channel_id=1, source_target_pairs={{0,16},{2,18},{4,20},{6,22},{8,24},{10,26},{12,28},{14,30},{16,0},... | collective-permute-start | bytes 184328 | tf_op jit(solution)/shard_map/ppermute | solution.py:654
  60.6 1.9 %collective-permute-start.5 = (bf16[8,240,128]{2,1,0:T(8,128)(2,1)S(1)}, bf16[8,240,128]{2,1,0:T(8,128)(2,1)S(1)}, u32[]{:S(2)}, u32[]{:S(2)}) collective-permute-start(bf16[8,240,128]{2,1,0:T(8,128)(2,1)S(1)} %all_to_all.11.mine_ref), channel_id=1, source_target_pairs={{0,1},{1,0},{2,3},{3,2},{4,5},{5,4},{6,7},{7,6},{8,9},{9,8},{10,11... | collective-permute-start | bytes 1474568 | tf_op jit(solution)/shard_map/ppermute | solution.py:675

commit v3 on v2

--- a/solution.py
+++ b/solution.py
@@ -162,10 +162,10 @@
 
 
 def forward_kernel(
-    scale, halo_ref, wide_ref, split_ref, part_ref, act_ref, k2t_ref, cot_ref,
-    grad_ref, p2_ref, slope_ref, cells_ref, *rest,
+    scale, halo_ref, wide_ref, split_ref, part_ref, act_ref, k2t_ref, cot_ref, rows_ref, p1_ref,
+    grad_ref, p2_ref, slope_ref, low_ref, *rest,
 ):
-    feat_refs, (rows_scr, lhs_scr, cells_scr, p2_scr, feat_scr) = rest[:-5], rest[-5:]
+    feat_refs, (rows_scr, lhs_scr, cells_scr, cells_ref, p2_scr, feat_scr) = rest[:-6], rest[-6:]
     channels, halo = halo_ref.shape[0], halo_ref.shape[1]
     planes = [halo_ref.at[c, z] for c in range(channels) for z in range(halo)]
     split_cells(planes, split_ref, cells_ref, rows_scr, lhs_scr, cells_scr)
@@ -177,9 +177,15 @@
     tall = part_ref.shape[0]
     hidden = tall // 4
     rows_two = hidden * TAPS
+    part, rows_pad, width = rows_ref.shape
+    both = jnp.concatenate([wide_ref[...], rows_ref[...].reshape(part * rows_pad, width)], axis=0)
+    product = dot(both, cells_ref[...])
+    for at in range(part):
+        start = 2 * tall + at * rows_pad
+        low_ref[at] = (product[start : start + rows_pad, :] + p1_ref[at].astype(F32)).astype(BF16)
     for j in (2, 1, 0):
         if j < 2:
-            pre = dot(wide_ref[j * tall : (j + 1) * tall, :], cells_ref[...])
+            pre = product[j * tall : (j + 1) * tall, :]
             if j == 1:
                 pre = pre + part_ref[...]
         for parity in range(4):
@@ -367,15 +373,10 @@
 
 
 def low_kernel(
-    grad_ref, back_ref, slope_ref, p1_ref, cells_ref, rows_ref, in_one_ref, done_ref,
+    grad_ref, back_ref, slope_ref, p1_ref, in_one_ref, done_ref,
     in_one_out, low_out, high_ref, scr,
 ):
-    _, rows_pad, _ = p1_ref.shape
-    part, _, width = rows_ref.shape
-    extra = dot(rows_ref[...].reshape(part * rows_pad, width), cells_ref[...])
-    p1 = [
-        (extra[at * rows_pad : (at + 1) * rows_pad, :] + p1_ref[at].astype(F32)).astype(BF16) for at in range(part)
-    ]
+    part, rows_pad, _ = p1_ref.shape
     shifted_up(grad_ref, scr)
     tall = high_ref.shape[0]
     hidden = tall // part
@@ -386,8 +387,8 @@
     for block in range(part):
         rows = slice(block * hidden, (block + 1) * hidden)
         piece = (grad_hidden[rows, :] * slope_ref[rows, :]).astype(BF16)
-        in_one += dot_nt(p1[block], p1[block])
-        total += dot_nt(piece, jnp.concatenate([p1[block], piece], axis=0))
+        in_one += dot_nt(p1_ref[block], p1_ref[block])
+        total += dot_nt(piece, jnp.concatenate([p1_ref[block], piece], axis=0))
     in_one_out[...] = in_one
     low_out[...] = total
 
@@ -731,19 +732,20 @@
     feat_tall = up_to(feat_rows, 16)
     cube = cube_size(space)
     cubes = space // cube
-    grad_two, p2, slope_low, spread, *feats = call(
+    grad_two, p2, slope_low, p1_low, *feats = call(
         functools.partial(forward_kernel, 1.0 / math.sqrt(total_two)),
         (
             like((out_chan, cells)),
             like((panels * LANES, cells)),
             like((tall, cells), F32),
-            like((halo_width, cells)),
+            like((4, rows_pad, cells)),
         )
         + (like((cube, feat_tall, LANES)),) * cubes,
         split_scratch(channels * halo, plane)
+        + [pltpu.VMEM((halo_width, cells), BF16)]
         + [pltpu.VMEM((rows_two * (cells // LANES) + 32, LANES), F32), pltpu.VMEM((space, feat_tall, LANES), BF16)],
         micros=5,
-    )(halo_block, halo_wide, split, part, act_high, kernel_two.T, cotangent.reshape(out_chan, cells))
+    )(halo_block, halo_wide, split, part, act_high, kernel_two.T, cotangent.reshape(out_chan, cells), halo_rows[4:], p1)
     feats = feats[:1] + [from_partner(feats[change], change * cube) for change in range(1, cubes)]
     above = passed_along(grad_two, "space", -1)
     feats, above = lax.optimization_barrier((feats, above))
@@ -763,7 +765,7 @@
         (like((rows_pad, rows_pad), F32), like((hidden, rows_pad + hidden), F32), like((tall, cells), F32)),
         [pltpu.VMEM((4 * out_chan, cells), BF16)],
         micros=0.1,
-    )(grad_two, back, slope_low, p1, spread, halo_rows[4:], in_one_part, done)
+    )(grad_two, back, slope_low, p1_low, in_one_part, done)
     small = call(
         high_kernel,
         like((small_rows, LANES)),

time: 64.6 us -> 64 us (level)
  transfers between devices with their start and end apart: 6 -> 6, of which waited for: 3 -> 3; matrix products, arithmetic and copies ran while one was open for 0% -> 0% of each run, Pallas kernels for 16% -> 15%
where the time goes in v3:
time: 64 us; the launch traced here: 63.5 us
  blocking collectives  23.2 us (36%)
  Pallas kernels  14.5 us (23%)
  starting transfers between devices  12.9 us (20%)
  waiting for transfers between devices  6.17 us (10%)
  local copies, waits for them, and re-layouts  6.05 us (9%)
  between operations  0.76 us (1%)
    all_to_all x2, blocking collectives, exchange(): lax.all_to_all(parts, 'space', split_axis=0, concat_axis=0, axis_index_gr...  23.2 us
    ppermute x2, starting transfers between devices, from_partner(): lax.ppermute(block, 'space', [(i, i ^ stride) for i in range(lax.axis_siz...  6.64 us
    ppermute x2, starting transfers between devices, passed_along(): return lax.ppermute(block, axis, route)  6.16 us
    ppermute x2, waiting for transfers between devices, from_partner(): lax.ppermute(block, 'space', [(i, i ^ stride) for i in range(lax.axis_siz...  5.73 us
    unnamed x20, local copies, waits for them, and re-layouts  5.02 us
    pallas_call x1, Pallas kernels, local(): call(own_kernel, (like((tall, cells), F32), like((tall, cells), F32), lik...  3.17 us
    pallas_call x1, Pallas kernels, local(): call(functools.partial(forward_kernel, 1.0 / math.sqrt(total_two)), (like...  2.79 us
    pallas_call x1, Pallas kernels, local(): call(functools.partial(sums_kernel, places, rows_two), (like((half, LANES...  2.15 us
  transfers between devices with their start and end apart: 6, of which 3 were waited for; matrix products, arithmetic and copies ran while one was open for 0% of the time, Pallas kernels for 15%

profile of v3, /device:TPU:0, one launch (start us, length us, event | category | flops | bytes accessed | tf_op | source)
XLA Modules:
  0.0 63.5 jit_solution(17524412051378723264)
XLA Ops:
  0.6 1.0 %slice.8 = bf16[4,3,128,128]{3,2,1,0:T(8,128)(2,1)S(1)} slice(bf16[4,4,128,128]{3,2,1,0:T(8,128)(2,1)} %bitcast.9), slice={[0:4], [1:4], [0:128], [0:128]} | slice | bytes 786432 | tf_op jit(solution)/shard_map/slice | solution.py:708
  1.7 4.9 %collective-permute-start = (bf16[4,3,128,128]{3,2,1,0:T(8,128)(2,1)S(1)}, bf16[4,3,128,128]{3,2,1,0:T(8,128)(2,1)S(1)}, u32[]{:S(2)}, u32[]{:S(2)}) collective-permute-start(bf16[4,3,128,128]{3,2,1,0:T(8,128)(2,1)S(1)} %slice.8), channel_id=1, source_target_pairs={{0,2},{2,4},{4,6},{6,8},{8,10},{10,12},{12,14},{14,16},{16,18},{18... | collective-permute-start | bytes 1179656 | tf_op jit(solution)/shard_map/ppermute | solution.py:672
  6.5 0.0 copy-start.2
  6.6 0.9 %copy-done.2 = bf16[864,64]{0,1:T(8,128)(2,1)S(1)} copy-done((bf16[864,64]{0,1:T(8,128)(2,1)S(1)}, bf16[864,64]{0,1:T(8,128)(2,1)}, u32[]{:S(2)}) %copy-start.2) | copy-done | bytes 110616
  7.4 0.7 %copy-done.4 = bf16[108,32]{0,1:T(8,128)(2,1)S(1)} copy-done((bf16[108,32]{0,1:T(8,128)(2,1)S(1)}, bf16[108,32]{0,1:T(8,128)(2,1)}, u32[]{:S(2)}) %copy-start.4) | copy-done | bytes 6936
  8.1 1.2 %copy-done.5 = bf16[8,112,400]{2,1,0:T(8,128)(2,1)S(1)} copy-done((bf16[8,112,400]{2,1,0:T(8,128)(2,1)S(1)}, bf16[8,112,400]{2,1,0:T(8,128)(2,1)}, u32[]{:S(2)}) %copy-start.5) | copy-done | bytes 716824
  9.3 1.1 %copy-done.7 = bf16[8,112,304]{2,1,0:T(8,128)(2,1)S(1)} copy-done((bf16[8,112,304]{2,1,0:T(8,128)(2,1)S(1)}, bf16[8,112,304]{2,1,0:T(8,128)(2,1)}, u32[]{:S(2)}) %copy-start.7) | copy-done | bytes 544792
  10.4 0.4 shard_map.126
  10.8 0.7 %copy-done = bf16[4,1,4,128,128]{4,3,2,1,0:T(8,128)(2,1)S(1)} copy-done((bf16[4,1,4,128,128]{4,3,2,1,0:T(8,128)(2,1)S(1)}, bf16[4,1,4,128,128]{4,3,2,1,0:T(8,128)(2,1)}, u32[]{:S(2)}) %copy-start) | copy-done | bytes 524312
  11.5 0.3 copy-done.6
  11.8 0.2 copy-done.8
  11.9 3.2 %shard_map.127 = (f32[128,1024]{1,0:T(8,128)S(1)}, f32[128,1024]{1,0:T(8,128)S(1)}, f32[128,1024]{1,0:T(8,128)S(1)}, bf16[8,112,1024]{2,1,0:T(8,128)(2,1)S(1)}, f32[112,112]{1,0:T(8,128)S(1)}) custom-call(bf16[4,4,128,128]{3,2,1,0:T(8,128)(2,1)S(1)} %bitcast.10, bf16[256,400]{1,0:T(8,128)(2,1)S(1)} %get-tuple-element.41.wide_ref, ...), custom_call_target="tpu_custom_call" | custom-call | flops 6600000000 | bytes 1048576 | tf_op jit(solution)/shard_map/pallas_call | solution.py:718
  15.1 0.0 collective-permute-done.halo_ref
  15.2 2.8 %shard_map.128 = (bf16[64,1024]{1,0:T(8,128)(2,1)S(1)}, bf16[896,1024]{1,0:T(8,128)(2,1)S(1)}, f32[128,1024]{1,0:T(8,128)S(1)}, bf16[4,112,1024]{2,1,0:T(8,128)(...) custom-call(bf16[4,3,128,128]{3,2,1,0:T(8,128)(2,1)S(1)} %collective-permute-done.halo_ref, ...), custom_call_target="tpu_custom_call" | custom-call | flops 5500000256 | bytes 1048576 | tf_op jit(solution)/shard_map/pallas_call | solution.py:735
  18.0 1.3 %collective-permute-start.3 = (bf16[64,1024]{1,0:T(8,128)(2,1)S(1)}, bf16[64,1024]{1,0:T(8,128)(2,1)S(1)}, u32[]{:S(2)}, u32[]{:S(2)}) collective-permute-start(bf16[64,1024]{1,0:T(8,128)(2,1)S(1)} %get-tuple-element.46.grad_ref), channel_id=1, source_target_pairs={{2,0},{4,2},{6,4},{8,6},{10,8},{12,10},{14,12},{16,14},{18,16},{20... | collective-permute-start | bytes 393224 | tf_op jit(solution)/shard_map/ppermute | solution.py:672
  19.3 6.3 %collective-permute-start.2 = (bf16[8,32,128]{2,1,0:T(8,128)(2,1)S(1)}, bf16[8,32,128]{2,1,0:T(8,128)(2,1)S(1)}, u32[]{:S(2)}, u32[]{:S(2)}) collective-permute-start(bf16[8,32,128]{2,1,0:T(8,128)(2,1)S(1)} %get-tuple-element.50), channel_id=1, source_target_pairs={{0,16},{2,18},{4,20},{6,22},{8,24},{10,26},{12,28},{14,30},{16,0},... | collective-permute-start | bytes 196616 | tf_op jit(solution)/shard_map/ppermute | solution.py:655
  25.6 2.2 %shard_map.129 = (bf16[1792,128]{1,0:T(8,128)(2,1)S(1)}, bf16[1792,128]{1,0:T(8,128)(2,1)S(1)}, f32[8,128]{1,0:T(8,128)S(1)}) custom-call(bf16[896,1024]{1,0:T(8,128)(2,1)S(1)} %get-tuple-element.45.p2_ref, bf16[64,1024]{1,0:T(8,128)(2,1)S(1)} %get-tuple-element.46.grad_ref), custom_call_target="tpu_custom_call" | custom-call | flops 110000000 | bytes 1048576 | tf_op jit(solution)/shard_map/pallas_call | solution.py:756
  27.7 0.1 collective-permute-start.1
  27.8 1.0 %shard_map.130 = (f32[112,112]{1,0:T(8,128)S(1)}, f32[32,144]{1,0:T(8,128)S(1)}, f32[128,1024]{1,0:T(8,128)S(1)}) custom-call(bf16[64,1024]{1,0:T(8,128)(2,1)S(1)} %get-tuple-element.46.grad_ref, bf16[256,512]{1,0:T(8,128)(2,1)S(1)} %get-tuple-element.52.back_ref, f32[128,1024]{1,0:T(8,128)S(1)} %get-tuple-element.53.slope_ref, ...), custom_call_target="tpu_custom_call" | custom-call | flops 110000000 | bytes 1048576 | tf_op jit(solution)/shard_map/pallas_call | solution.py:763
  28.8 1.8 %collective-permute-done.2.refs_1_ = bf16[8,32,128]{2,1,0:T(8,128)(2,1)S(1)} collective-permute-done((bf16[8,32,128]{2,1,0:T(8,128)(2,1)S(1)}, bf16[8,32,128]{2,1,0:T(8,128)(2,1)S(1)}, u32[]{:S(2)}, u32[]{:S(2)}) %collective-permute-start.2) | collective-permute-done | bytes 65568 | tf_op jit(solution)/shard_map/ppermute | solution.py:655
  30.6 0.0 collective-permute-done.3.above_ref
  30.6 0.7 %shard_map.131.small_ref = bf16[128,128]{1,0:T(8,128)(2,1)S(1)} custom-call(bf16[64,1024]{1,0:T(8,128)(2,1)S(1)} %collective-permute-done.3.above_ref, bf16[256,512]{1,0:T(8,128)(2,1)S(1)} %get-tuple-element.52.back_ref, f32[128,1024]{1,0:T(8,128)S(1)} %get-tuple-element.57.high_ref, f32[128,1024]{1,0:T(8,128)S(1)} %get-tuple-element.58.slope_ref, ...), custom_call_target="tpu_custom_call" | custom-call | flops 13200000000 | bytes 1048576 | tf_op jit(solution)/shard_map/pallas_call | solution.py:769
  31.4 0.1 shard_map.132
  31.5 13.0 %all_to_all.10.came_ref = bf16[8,304,128]{2,1,0:T(8,128)(2,1)S(1)} all-to-all(bf16[8,304,128]{2,1,0:T(8,128)(2,1)S(1)} %shard_map.132), channel_id=1, replica_groups={{0,2,6,4,12,14,10,8},{16,18,22,20,28,30,26,24},{1,3,7,5,13,15,11,9},{17..., dimensions={0} | all-to-all | bytes 1245184 | tf_op jit(solution)/shard_map/all_to_all | solution.py:651
  44.5 0.1 shard_map.133
  44.5 0.3 collective-permute-start.4
  44.9 1.0 %shard_map.134 = bf16[64,16,64]{2,1,0:T(8,128)(2,1)} custom-call(bf16[8,64,128]{2,1,0:T(8,128)(2,1)S(1)} %get-tuple-element.64.feat_ref), custom_call_target="tpu_custom_call" | custom-call | flops 1100000000 | bytes 1048576 | tf_op jit(solution)/shard_map/pallas_call | solution.py:783
  45.8 3.9 %collective-permute-done.4.came_ref = bf16[240,128]{1,0:T(8,128)(2,1)S(1)} collective-permute-done((bf16[240,128]{1,0:T(8,128)(2,1)S(1)}, bf16[240,128]{1,0:T(8,128)(2,1)S(1)}, u32[]{:S(2)}, u32[]{:S(2)}) %collective-permute-start.4) | collective-permute-done | bytes 61472 | tf_op jit(solution)/shard_map/ppermute | solution.py:655
  49.8 10.3 %all_to_all.11.mine_ref = bf16[8,240,128]{2,1,0:T(8,128)(2,1)S(1)} all-to-all(bf16[8,240,128]{2,1,0:T(8,128)(2,1)S(1)} %shard_map.135), channel_id=1, replica_groups={{0,2,6,4,12,14,10,8},{16,18,22,20,28,30,26,24},{1,3,7,5,13,15,11,9},{17..., dimensions={0} | all-to-all | bytes 983040 | tf_op jit(solution)/shard_map/all_to_all | solution.py:651
  60.0 1.4 %shard_map.136.begun_ref = f32[864,864]{1,0:T(8,128)} custom-call(bf16[8,240,128]{2,1,0:T(8,128)(2,1)S(1)} %all_to_all.11.mine_ref), custom_call_target="tpu_custom_call" | custom-call | flops 2200000000 | bytes 1048576 | tf_op jit(solution)/shard_map/pallas_call | solution.py:795
  61.5 0.4 collective-permute-done.5.came_ref
  61.9 1.7 %shard_map.137 = (f32[108,108]{1,0:T(8,128)}, f32[864,864]{1,0:T(8,128)}, f32[32,32]{1,0:T(8,128)}, f32[64,64]{1,0:T(8,128)}, f32[32,108]{1,0:T(8,128)}, /*index=5*/f32[64,864]{1,0:T(8,128)}) custom-call(f32[864,864]{1,0:T(8,128)} %shard_map.136.begun_ref, bf16[8,240,128]{2,1,0:T(8,128)(2,1)S(1)} %all_to_all.11.mine_ref, ...), custom_call_target="tpu_custom_call", output_to_operand_aliasing={{1}: (0, {})} | custom-call | flops 2200000000 | bytes 1048576 | tf_op jit(solution)/shard_map/pallas_call | solution.py:817
  (15 shorter events, 0.1 us)
Async XLA Ops:
  1.7 13.5 %collective-permute-start = (bf16[4,3,128,128]{3,2,1,0:T(8,128)(2,1)S(1)}, bf16[4,3,128,128]{3,2,1,0:T(8,128)(2,1)S(1)}, u32[]{:S(2)}, u32[]{:S(2)}) collective-permute-start(bf16[4,3,128,128]{3,2,1,0:T(8,128)(2,1)S(1)} %slice.8), channel_id=1, source_target_pairs={{0,2},{2,4},{4,6},{6,8},{8,10},{10,12},{12,14},{14,16},{16,18},{18... | collective-permute-start | bytes 1179656 | tf_op jit(solution)/shard_map/ppermute | solution.py:672
  6.5 0.9 %copy-start.2 = (bf16[864,64]{0,1:T(8,128)(2,1)S(1)}, bf16[864,64]{0,1:T(8,128)(2,1)}, u32[]{:S(2)}) copy-start(bf16[864,64]{0,1:T(8,128)(2,1)} %param.9) | copy-start | bytes 331780
  7.4 0.7 %copy-start.4 = (bf16[108,32]{0,1:T(8,128)(2,1)S(1)}, bf16[108,32]{0,1:T(8,128)(2,1)}, u32[]{:S(2)}) copy-start(bf16[108,32]{0,1:T(8,128)(2,1)} %param.8) | copy-start | bytes 20740
  8.1 1.2 %copy-start.5 = (bf16[8,112,400]{2,1,0:T(8,128)(2,1)S(1)}, bf16[8,112,400]{2,1,0:T(8,128)(2,1)}, u32[]{:S(2)}) copy-start(bf16[8,112,400]{2,1,0:T(8,128)(2,1)} %constant.7.clone.own_rows_ref.rows_ref) | copy-start | bytes 2150404
  9.3 1.1 %copy-start.7 = (bf16[8,112,304]{2,1,0:T(8,128)(2,1)S(1)}, bf16[8,112,304]{2,1,0:T(8,128)(2,1)}, u32[]{:S(2)}) copy-start(bf16[8,112,304]{2,1,0:T(8,128)(2,1)} %constant.6.clone.halo_rows_ref) | copy-start | bytes 1634308
  10.4 1.0 %copy-start = (bf16[4,1,4,128,128]{4,3,2,1,0:T(8,128)(2,1)S(1)}, bf16[4,1,4,128,128]{4,3,2,1,0:T(8,128)(2,1)}, u32[]{:S(2)}) copy-start(bf16[4,1,4,128,128]{4,3,2,1,0:T(8,128)(2,1)} %param.7) | copy-start | bytes 1572868
  10.4 1.3 %copy-start.6 = (bf16[8,112,400]{2,1,0:T(8,128)(2,1)S(1)}, bf16[8,112,400]{2,1,0:T(8,128)(2,1)}, u32[]{:S(2)}) copy-start(bf16[8,112,400]{2,1,0:T(8,128)(2,1)} %constant.7.clone.own_rows_ref.rows_ref) | copy-start | bytes 2150404
  10.4 1.5 %copy-start.8 = (bf16[512,640]{1,0:T(8,128)(2,1)S(1)}, bf16[512,640]{1,0:T(8,128)(2,1)}, u32[]{:S(2)}) copy-start(bf16[512,640]{1,0:T(8,128)(2,1)} %constant.8.clone.split_ref) | copy-start | bytes 1966084
  11.9 3.2 %copy-start.1 = (bf16[64,1,1,1024]{3,0,2,1:T(8,128)(2,1)S(1)}, bf16[64,1,1,1024]{3,0,2,1:T(8,128)(2,1)}, u32[]{:S(2)}) copy-start(bf16[64,1,1,1024]{3,0,2,1:T(8,128)(2,1)} %param.10) | copy-start | bytes 393220
  11.9 3.2 %copy-start.3 = (bf16[864,64]{0,1:T(8,128)(2,1)S(1)}, bf16[864,64]{0,1:T(8,128)(2,1)}, u32[]{:S(2)}) copy-start(bf16[864,64]{0,1:T(8,128)(2,1)} %param.9) | copy-start | bytes 331780
  11.9 3.2 %copy-start.9 = (bf16[4,112,304]{2,1,0:T(8,128)(2,1)S(1)}, bf16[4,112,304]{2,1,0:T(8,128)(2,1)}, u32[]{:S(2)}) copy-start(bf16[4,112,304]{2,1,0:T(8,128)(2,1)} %constant.11.rows_ref) | copy-start | bytes 817156
  18.0 12.7 %collective-permute-start.3 = (bf16[64,1024]{1,0:T(8,128)(2,1)S(1)}, bf16[64,1024]{1,0:T(8,128)(2,1)S(1)}, u32[]{:S(2)}, u32[]{:S(2)}) collective-permute-start(bf16[64,1024]{1,0:T(8,128)(2,1)S(1)} %get-tuple-element.46.grad_ref), channel_id=1, source_target_pairs={{2,0},{4,2},{6,4},{8,6},{10,8},{12,10},{14,12},{16,14},{18,16},{20... | collective-permute-start | bytes 393224 | tf_op jit(solution)/shard_map/ppermute | solution.py:672
  19.3 11.4 %collective-permute-start.2 = (bf16[8,32,128]{2,1,0:T(8,128)(2,1)S(1)}, bf16[8,32,128]{2,1,0:T(8,128)(2,1)S(1)}, u32[]{:S(2)}, u32[]{:S(2)}) collective-permute-start(bf16[8,32,128]{2,1,0:T(8,128)(2,1)S(1)} %get-tuple-element.50), channel_id=1, source_target_pairs={{0,16},{2,18},{4,20},{6,22},{8,24},{10,26},{12,28},{14,30},{16,0},... | collective-permute-start | bytes 196616 | tf_op jit(solution)/shard_map/ppermute | solution.py:655
  27.7 3.7 %collective-permute-start.1 = (bf16[1792,128]{1,0:T(8,128)(2,1)S(1)}, bf16[1792,128]{1,0:T(8,128)(2,1)S(1)}, u32[]{:S(2)}, u32[]{:S(2)}) collective-permute-start(bf16[1792,128]{1,0:T(8,128)(2,1)S(1)} %get-tuple-element.48), channel_id=1, source_target_pairs={{0,1},{1,0},{2,3},{3,2},{4,5},{5,4},{6,7},{7,6},{8,9},{9,8},{10,11... | collective-permute-start | bytes 1376264 | tf_op jit(solution)/shard_map/ppermute | solution.py:676
  44.5 5.2 %collective-permute-start.4 = (bf16[240,128]{1,0:T(8,128)(2,1)S(1)}, bf16[240,128]{1,0:T(8,128)(2,1)S(1)}, u32[]{:S(2)}, u32[]{:S(2)}) collective-permute-start(bf16[240,128]{1,0:T(8,128)(2,1)S(1)} %get-tuple-element.63.mine_ref), channel_id=1, source_target_pairs={{0,16},{2,18},{4,20},{6,22},{8,24},{10,26},{12,28},{14,30},{16,0},... | collective-permute-start | bytes 184328 | tf_op jit(solution)/shard_map/ppermute | solution.py:655
  60.0 1.9 %collective-permute-start.5 = (bf16[8,240,128]{2,1,0:T(8,128)(2,1)S(1)}, bf16[8,240,128]{2,1,0:T(8,128)(2,1)S(1)}, u32[]{:S(2)}, u32[]{:S(2)}) collective-permute-start(bf16[8,240,128]{2,1,0:T(8,128)(2,1)S(1)} %all_to_all.11.mine_ref), channel_id=1, source_target_pairs={{0,1},{1,0},{2,3},{3,2},{4,5},{5,4},{6,7},{7,6},{8,9},{9,8},{10,11... | collective-permute-start | bytes 1474568 | tf_op jit(solution)/shard_map/ppermute | solution.py:676

commit v4 on v3

--- a/solution.py
+++ b/solution.py
@@ -444,18 +444,25 @@
     return in_one, weight_one[:, :rows_one], out_one
 
 
-def joined_kernel(mine_ref, came_ref, small_ref, *refs):
+def tail_kernel(small_ref, *refs):
     feat_refs, out_ref = refs[:-1], refs[-1]
     owners = out_ref.shape[0]
-    large, small = mine_ref.shape[0] // owners, small_ref.shape[0] // owners
+    small = small_ref.shape[0] // owners
     feat_rows = feat_refs[0].shape[1]
+    for owner in range(owners):
+        out_ref[owner, :small, :] = small_ref[owner * small : (owner + 1) * small, :]
+        for change, feat_ref in enumerate(feat_refs):
+            start = small + change * feat_rows
+            out_ref[owner, start : start + feat_rows, :] = feat_ref[walk(owners)[owner]]
+
+
+def joined_kernel(mine_ref, came_ref, tail_ref, out_ref):
+    owners = out_ref.shape[0]
+    large = mine_ref.shape[0] // owners
     for owner in range(owners):
         rows = slice(owner * large, (owner + 1) * large)
         out_ref[owner, :large, :] = (mine_ref[rows, :].astype(F32) + came_ref[rows, :].astype(F32)).astype(BF16)
-        out_ref[owner, large : large + small, :] = small_ref[owner * small : (owner + 1) * small, :]
-        for change, feat_ref in enumerate(feat_refs):
-            start = large + small + change * feat_rows
-            out_ref[owner, start : start + feat_rows, :] = feat_ref[walk(owners)[owner]]
+        out_ref[owner, large:, :] = tail_ref[owner]
 
 
 def total_kernel(came_ref, out_ref, feat_ref):
@@ -748,7 +755,6 @@
     )(halo_block, halo_wide, split, part, act_high, kernel_two.T, cotangent.reshape(out_chan, cells), halo_rows[4:], p1)
     feats = feats[:1] + [from_partner(feats[change], change * cube) for change in range(1, cubes)]
     above = passed_along(grad_two, "space", -1)
-    feats, above = lax.optimization_barrier((feats, above))
 
     half = large_rows // 2
     small_rows = LANES
@@ -770,9 +776,12 @@
         high_kernel,
         like((small_rows, LANES)),
         [pltpu.VMEM((4 * out_chan, cells), BF16)],
-        micros=12,
+        micros=0.1,
     )(above, back, high, slope_high, p1, in_one_low, low)
-    joined = call(joined_kernel, like((cube, chunk + cubes * feat_tall, LANES)), micros=1)(mine, came, small, *feats)
+    tail = call(
+        tail_kernel, like((cube, small_rows // cube + cubes * feat_tall, LANES)), micros=12
+    )(small, *feats)
+    joined = call(joined_kernel, like((cube, chunk + cubes * feat_tall, LANES)), micros=1)(mine, came, tail)
     total, feat = call(
         total_kernel, (like((chunk, LANES)), like((cube, cubes * feat_tall, LANES))), micros=1
     )(exchange(joined, cube))

time: 64 us -> 64.3 us (level)
  no operation moved by 1% of the time
where the time goes in v4:
time: 64.3 us; the launch traced here: 63.9 us
  blocking collectives  23.7 us (37%)
  Pallas kernels  14.5 us (23%)
  starting transfers between devices  12.9 us (20%)
  local copies, waits for them, and re-layouts  6.05 us (9%)
  waiting for transfers between devices  5.99 us (9%)
  between operations  0.77 us (1%)
    all_to_all x2, blocking collectives, exchange(): lax.all_to_all(parts, 'space', split_axis=0, concat_axis=0, axis_index_gr...  23.7 us
    ppermute x2, starting transfers between devices, from_partner(): lax.ppermute(block, 'space', [(i, i ^ stride) for i in range(lax.axis_siz...  6.7 us
    ppermute x2, starting transfers between devices, passed_along(): return lax.ppermute(block, axis, route)  6.16 us
    ppermute x2, waiting for transfers between devices, from_partner(): lax.ppermute(block, 'space', [(i, i ^ stride) for i in range(lax.axis_siz...  5.55 us
    unnamed x20, local copies, waits for them, and re-layouts  5.02 us
    pallas_call x1, Pallas kernels, local(): call(own_kernel, (like((tall, cells), F32), like((tall, cells), F32), lik...  3.18 us
    pallas_call x1, Pallas kernels, local(): call(functools.partial(forward_kernel, 1.0 / math.sqrt(total_two)), (like...  2.75 us
    pallas_call x1, Pallas kernels, local(): call(functools.partial(sums_kernel, places, rows_two), (like((half, LANES...  2.15 us
  transfers between devices with their start and end apart: 6, of which 3 were waited for; matrix products, arithmetic and copies ran while one was open for 0% of the time, Pallas kernels for 15%

profile of v4, /device:TPU:0, one launch (start us, length us, event | category | flops | bytes accessed | tf_op | source)
XLA Modules:
  0.0 63.9 jit_solution(4194919409793011300)
XLA Ops:
  0.6 1.0 %slice.8 = bf16[4,3,128,128]{3,2,1,0:T(8,128)(2,1)S(1)} slice(bf16[4,4,128,128]{3,2,1,0:T(8,128)(2,1)} %bitcast.9), slice={[0:4], [1:4], [0:128], [0:128]} | slice | bytes 786432 | tf_op jit(solution)/shard_map/slice | solution.py:715
  1.7 4.9 %collective-permute-start = (bf16[4,3,128,128]{3,2,1,0:T(8,128)(2,1)S(1)}, bf16[4,3,128,128]{3,2,1,0:T(8,128)(2,1)S(1)}, u32[]{:S(2)}, u32[]{:S(2)}) collective-permute-start(bf16[4,3,128,128]{3,2,1,0:T(8,128)(2,1)S(1)} %slice.8), channel_id=1, source_target_pairs={{0,2},{2,4},{4,6},{6,8},{8,10},{10,12},{12,14},{14,16},{16,18},{18... | collective-permute-start | bytes 1179656 | tf_op jit(solution)/shard_map/ppermute | solution.py:679
  6.5 0.0 copy-start.2
  6.6 0.9 %copy-done.2 = bf16[864,64]{0,1:T(8,128)(2,1)S(1)} copy-done((bf16[864,64]{0,1:T(8,128)(2,1)S(1)}, bf16[864,64]{0,1:T(8,128)(2,1)}, u32[]{:S(2)}) %copy-start.2) | copy-done | bytes 110616
  7.4 0.7 %copy-done.4 = bf16[108,32]{0,1:T(8,128)(2,1)S(1)} copy-done((bf16[108,32]{0,1:T(8,128)(2,1)S(1)}, bf16[108,32]{0,1:T(8,128)(2,1)}, u32[]{:S(2)}) %copy-start.4) | copy-done | bytes 6936
  8.1 1.2 %copy-done.5 = bf16[8,112,400]{2,1,0:T(8,128)(2,1)S(1)} copy-done((bf16[8,112,400]{2,1,0:T(8,128)(2,1)S(1)}, bf16[8,112,400]{2,1,0:T(8,128)(2,1)}, u32[]{:S(2)}) %copy-start.5) | copy-done | bytes 716824
  9.3 1.1 %copy-done.7 = bf16[8,112,304]{2,1,0:T(8,128)(2,1)S(1)} copy-done((bf16[8,112,304]{2,1,0:T(8,128)(2,1)S(1)}, bf16[8,112,304]{2,1,0:T(8,128)(2,1)}, u32[]{:S(2)}) %copy-start.7) | copy-done | bytes 544792
  10.4 0.4 shard_map.126
  10.8 0.7 %copy-done = bf16[4,1,4,128,128]{4,3,2,1,0:T(8,128)(2,1)S(1)} copy-done((bf16[4,1,4,128,128]{4,3,2,1,0:T(8,128)(2,1)S(1)}, bf16[4,1,4,128,128]{4,3,2,1,0:T(8,128)(2,1)}, u32[]{:S(2)}) %copy-start) | copy-done | bytes 524312
  11.5 0.3 copy-done.6
  11.8 0.2 copy-done.8
  11.9 3.2 %shard_map.127 = (f32[128,1024]{1,0:T(8,128)S(1)}, f32[128,1024]{1,0:T(8,128)S(1)}, f32[128,1024]{1,0:T(8,128)S(1)}, bf16[8,112,1024]{2,1,0:T(8,128)(2,1)S(1)}, f32[112,112]{1,0:T(8,128)S(1)}) custom-call(bf16[4,4,128,128]{3,2,1,0:T(8,128)(2,1)S(1)} %bitcast.10, bf16[256,400]{1,0:T(8,128)(2,1)S(1)} %get-tuple-element.38.wide_ref, ...), custom_call_target="tpu_custom_call" | custom-call | flops 6600000000 | bytes 1048576 | tf_op jit(solution)/shard_map/pallas_call | solution.py:725
  15.1 0.0 collective-permute-done.halo_ref
  15.2 2.7 %shard_map.128 = (bf16[64,1024]{1,0:T(8,128)(2,1)S(1)}, bf16[896,1024]{1,0:T(8,128)(2,1)S(1)}, f32[128,1024]{1,0:T(8,128)S(1)}, bf16[4,112,1024]{2,1,0:T(8,128)(...) custom-call(bf16[4,3,128,128]{3,2,1,0:T(8,128)(2,1)S(1)} %collective-permute-done.halo_ref, ...), custom_call_target="tpu_custom_call" | custom-call | flops 5500000256 | bytes 1048576 | tf_op jit(solution)/shard_map/pallas_call | solution.py:742
  17.9 1.3 %collective-permute-start.2 = (bf16[64,1024]{1,0:T(8,128)(2,1)S(1)}, bf16[64,1024]{1,0:T(8,128)(2,1)S(1)}, u32[]{:S(2)}, u32[]{:S(2)}) collective-permute-start(bf16[64,1024]{1,0:T(8,128)(2,1)S(1)} %get-tuple-element.43.grad_ref), channel_id=1, source_target_pairs={{2,0},{4,2},{6,4},{8,6},{10,8},{12,10},{14,12},{16,14},{18,16},{20... | collective-permute-start | bytes 393224 | tf_op jit(solution)/shard_map/ppermute | solution.py:679
  19.2 6.3 %collective-permute-start.3 = (bf16[8,32,128]{2,1,0:T(8,128)(2,1)S(1)}, bf16[8,32,128]{2,1,0:T(8,128)(2,1)S(1)}, u32[]{:S(2)}, u32[]{:S(2)}) collective-permute-start(bf16[8,32,128]{2,1,0:T(8,128)(2,1)S(1)} %get-tuple-element.56), channel_id=1, source_target_pairs={{0,16},{2,18},{4,20},{6,22},{8,24},{10,26},{12,28},{14,30},{16,0},... | collective-permute-start | bytes 196616 | tf_op jit(solution)/shard_map/ppermute | solution.py:662
  25.5 2.2 %shard_map.129 = (bf16[1792,128]{1,0:T(8,128)(2,1)S(1)}, bf16[1792,128]{1,0:T(8,128)(2,1)S(1)}, f32[8,128]{1,0:T(8,128)S(1)}) custom-call(bf16[896,1024]{1,0:T(8,128)(2,1)S(1)} %get-tuple-element.42.p2_ref, bf16[64,1024]{1,0:T(8,128)(2,1)S(1)} %get-tuple-element.43.grad_ref), custom_call_target="tpu_custom_call" | custom-call | flops 110000000 | bytes 1048576 | tf_op jit(solution)/shard_map/pallas_call | solution.py:762
  27.7 0.1 collective-permute-start.1
  27.8 1.0 %shard_map.130 = (f32[112,112]{1,0:T(8,128)S(1)}, f32[32,144]{1,0:T(8,128)S(1)}, f32[128,1024]{1,0:T(8,128)S(1)}) custom-call(bf16[64,1024]{1,0:T(8,128)(2,1)S(1)} %get-tuple-element.43.grad_ref, bf16[256,512]{1,0:T(8,128)(2,1)S(1)} %get-tuple-element.46.back_ref, f32[128,1024]{1,0:T(8,128)S(1)} %get-tuple-element.47.slope_ref, ...), custom_call_target="tpu_custom_call" | custom-call | flops 110000000 | bytes 1048576 | tf_op jit(solution)/shard_map/pallas_call | solution.py:769
  28.8 0.0 collective-permute-done.2.above_ref
  28.8 0.8 %shard_map.131.small_ref = bf16[128,128]{1,0:T(8,128)(2,1)S(1)} custom-call(bf16[64,1024]{1,0:T(8,128)(2,1)S(1)} %collective-permute-done.2.above_ref, bf16[256,512]{1,0:T(8,128)(2,1)S(1)} %get-tuple-element.46.back_ref, f32[128,1024]{1,0:T(8,128)S(1)} %get-tuple-element.51.high_ref, f32[128,1024]{1,0:T(8,128)S(1)} %get-tuple-element.52.slope_ref, ...), custom_call_target="tpu_custom_call" | custom-call | flops 110000000 | bytes 1048576 | tf_op jit(solution)/shard_map/pallas_call | solution.py:775
  29.5 1.1 %collective-permute-done.3.refs_1_ = bf16[8,32,128]{2,1,0:T(8,128)(2,1)S(1)} collective-permute-done((bf16[8,32,128]{2,1,0:T(8,128)(2,1)S(1)}, bf16[8,32,128]{2,1,0:T(8,128)(2,1)S(1)}, u32[]{:S(2)}, u32[]{:S(2)}) %collective-permute-start.3) | collective-permute-done | bytes 65568 | tf_op jit(solution)/shard_map/ppermute | solution.py:662
  30.6 0.1 shard_map.133
  30.7 13.7 %all_to_all.10.came_ref = bf16[8,304,128]{2,1,0:T(8,128)(2,1)S(1)} all-to-all(bf16[8,304,128]{2,1,0:T(8,128)(2,1)S(1)} %shard_map.133), channel_id=1, replica_groups={{0,2,6,4,12,14,10,8},{16,18,22,20,28,30,26,24},{1,3,7,5,13,15,11,9},{17..., dimensions={0} | all-to-all | bytes 1245184 | tf_op jit(solution)/shard_map/all_to_all | solution.py:658
  44.4 0.1 shard_map.134
  44.5 0.4 collective-permute-start.4
  44.9 1.0 %shard_map.135 = bf16[64,16,64]{2,1,0:T(8,128)(2,1)} custom-call(bf16[8,64,128]{2,1,0:T(8,128)(2,1)S(1)} %get-tuple-element.58.feat_ref), custom_call_target="tpu_custom_call" | custom-call | flops 1100000000 | bytes 1048576 | tf_op jit(solution)/shard_map/pallas_call | solution.py:792
  45.8 4.5 %collective-permute-done.4.came_ref = bf16[240,128]{1,0:T(8,128)(2,1)S(1)} collective-permute-done((bf16[240,128]{1,0:T(8,128)(2,1)S(1)}, bf16[240,128]{1,0:T(8,128)(2,1)S(1)}, u32[]{:S(2)}, u32[]{:S(2)}) %collective-permute-start.4) | collective-permute-done | bytes 61472 | tf_op jit(solution)/shard_map/ppermute | solution.py:662
  50.4 10.0 %all_to_all.11.mine_ref = bf16[8,240,128]{2,1,0:T(8,128)(2,1)S(1)} all-to-all(bf16[8,240,128]{2,1,0:T(8,128)(2,1)S(1)} %shard_map.136), channel_id=1, replica_groups={{0,2,6,4,12,14,10,8},{16,18,22,20,28,30,26,24},{1,3,7,5,13,15,11,9},{17..., dimensions={0} | all-to-all | bytes 983040 | tf_op jit(solution)/shard_map/all_to_all | solution.py:658
  60.3 1.4 %shard_map.137.begun_ref = f32[864,864]{1,0:T(8,128)} custom-call(bf16[8,240,128]{2,1,0:T(8,128)(2,1)S(1)} %all_to_all.11.mine_ref), custom_call_target="tpu_custom_call" | custom-call | flops 2200000000 | bytes 1048576 | tf_op jit(solution)/shard_map/pallas_call | solution.py:804
  61.8 0.4 collective-permute-done.5.came_ref
  62.2 1.7 %shard_map.138 = (f32[108,108]{1,0:T(8,128)}, f32[864,864]{1,0:T(8,128)}, f32[32,32]{1,0:T(8,128)}, f32[64,64]{1,0:T(8,128)}, f32[32,108]{1,0:T(8,128)}, /*index=5*/f32[64,864]{1,0:T(8,128)}) custom-call(f32[864,864]{1,0:T(8,128)} %shard_map.137.begun_ref, bf16[8,240,128]{2,1,0:T(8,128)(2,1)S(1)} %all_to_all.11.mine_ref, ...), custom_call_target="tpu_custom_call", output_to_operand_aliasing={{1}: (0, {})} | custom-call | flops 2200000000 | bytes 1048576 | tf_op jit(solution)/shard_map/pallas_call | solution.py:826
  (16 shorter events, 0.1 us)
Async XLA Ops:
  1.7 13.5 %collective-permute-start = (bf16[4,3,128,128]{3,2,1,0:T(8,128)(2,1)S(1)}, bf16[4,3,128,128]{3,2,1,0:T(8,128)(2,1)S(1)}, u32[]{:S(2)}, u32[]{:S(2)}) collective-permute-start(bf16[4,3,128,128]{3,2,1,0:T(8,128)(2,1)S(1)} %slice.8), channel_id=1, source_target_pairs={{0,2},{2,4},{4,6},{6,8},{8,10},{10,12},{12,14},{14,16},{16,18},{18... | collective-permute-start | bytes 1179656 | tf_op jit(solution)/shard_map/ppermute | solution.py:679
  6.5 0.9 %copy-start.2 = (bf16[864,64]{0,1:T(8,128)(2,1)S(1)}, bf16[864,64]{0,1:T(8,128)(2,1)}, u32[]{:S(2)}) copy-start(bf16[864,64]{0,1:T(8,128)(2,1)} %param.9) | copy-start | bytes 331780
  7.4 0.7 %copy-start.4 = (bf16[108,32]{0,1:T(8,128)(2,1)S(1)}, bf16[108,32]{0,1:T(8,128)(2,1)}, u32[]{:S(2)}) copy-start(bf16[108,32]{0,1:T(8,128)(2,1)} %param.8) | copy-start | bytes 20740
  8.1 1.2 %copy-start.5 = (bf16[8,112,400]{2,1,0:T(8,128)(2,1)S(1)}, bf16[8,112,400]{2,1,0:T(8,128)(2,1)}, u32[]{:S(2)}) copy-start(bf16[8,112,400]{2,1,0:T(8,128)(2,1)} %constant.7.clone.own_rows_ref.rows_ref) | copy-start | bytes 2150404
  9.3 1.1 %copy-start.7 = (bf16[8,112,304]{2,1,0:T(8,128)(2,1)S(1)}, bf16[8,112,304]{2,1,0:T(8,128)(2,1)}, u32[]{:S(2)}) copy-start(bf16[8,112,304]{2,1,0:T(8,128)(2,1)} %constant.6.clone.halo_rows_ref) | copy-start | bytes 1634308
  10.4 1.0 %copy-start = (bf16[4,1,4,128,128]{4,3,2,1,0:T(8,128)(2,1)S(1)}, bf16[4,1,4,128,128]{4,3,2,1,0:T(8,128)(2,1)}, u32[]{:S(2)}) copy-start(bf16[4,1,4,128,128]{4,3,2,1,0:T(8,128)(2,1)} %param.7) | copy-start | bytes 1572868
  10.4 1.3 %copy-start.6 = (bf16[8,112,400]{2,1,0:T(8,128)(2,1)S(1)}, bf16[8,112,400]{2,1,0:T(8,128)(2,1)}, u32[]{:S(2)}) copy-start(bf16[8,112,400]{2,1,0:T(8,128)(2,1)} %constant.7.clone.own_rows_ref.rows_ref) | copy-start | bytes 2150404
  10.4 1.5 %copy-start.8 = (bf16[512,640]{1,0:T(8,128)(2,1)S(1)}, bf16[512,640]{1,0:T(8,128)(2,1)}, u32[]{:S(2)}) copy-start(bf16[512,640]{1,0:T(8,128)(2,1)} %constant.8.clone.split_ref) | copy-start | bytes 1966084
  11.9 3.2 %copy-start.1 = (bf16[64,1,1,1024]{3,0,2,1:T(8,128)(2,1)S(1)}, bf16[64,1,1,1024]{3,0,2,1:T(8,128)(2,1)}, u32[]{:S(2)}) copy-start(bf16[64,1,1,1024]{3,0,2,1:T(8,128)(2,1)} %param.10) | copy-start | bytes 393220
  11.9 3.2 %copy-start.3 = (bf16[864,64]{0,1:T(8,128)(2,1)S(1)}, bf16[864,64]{0,1:T(8,128)(2,1)}, u32[]{:S(2)}) copy-start(bf16[864,64]{0,1:T(8,128)(2,1)} %param.9) | copy-start | bytes 331780
  11.9 3.2 %copy-start.9 = (bf16[4,112,304]{2,1,0:T(8,128)(2,1)S(1)}, bf16[4,112,304]{2,1,0:T(8,128)(2,1)}, u32[]{:S(2)}) copy-start(bf16[4,112,304]{2,1,0:T(8,128)(2,1)} %constant.11.rows_ref) | copy-start | bytes 817156
  17.9 10.8 %collective-permute-start.2 = (bf16[64,1024]{1,0:T(8,128)(2,1)S(1)}, bf16[64,1024]{1,0:T(8,128)(2,1)S(1)}, u32[]{:S(2)}, u32[]{:S(2)}) collective-permute-start(bf16[64,1024]{1,0:T(8,128)(2,1)S(1)} %get-tuple-element.43.grad_ref), channel_id=1, source_target_pairs={{2,0},{4,2},{6,4},{8,6},{10,8},{12,10},{14,12},{16,14},{18,16},{20... | collective-permute-start | bytes 393224 | tf_op jit(solution)/shard_map/ppermute | solution.py:679
  19.2 11.4 %collective-permute-start.3 = (bf16[8,32,128]{2,1,0:T(8,128)(2,1)S(1)}, bf16[8,32,128]{2,1,0:T(8,128)(2,1)S(1)}, u32[]{:S(2)}, u32[]{:S(2)}) collective-permute-start(bf16[8,32,128]{2,1,0:T(8,128)(2,1)S(1)} %get-tuple-element.56), channel_id=1, source_target_pairs={{0,16},{2,18},{4,20},{6,22},{8,24},{10,26},{12,28},{14,30},{16,0},... | collective-permute-start | bytes 196616 | tf_op jit(solution)/shard_map/ppermute | solution.py:662
  27.7 2.9 %collective-permute-start.1 = (bf16[1792,128]{1,0:T(8,128)(2,1)S(1)}, bf16[1792,128]{1,0:T(8,128)(2,1)S(1)}, u32[]{:S(2)}, u32[]{:S(2)}) collective-permute-start(bf16[1792,128]{1,0:T(8,128)(2,1)S(1)} %get-tuple-element.45), channel_id=1, source_target_pairs={{0,1},{1,0},{2,3},{3,2},{4,5},{5,4},{6,7},{7,6},{8,9},{9,8},{10,11... | collective-permute-start | bytes 1376264 | tf_op jit(solution)/shard_map/ppermute | solution.py:683
  44.5 5.8 %collective-permute-start.4 = (bf16[240,128]{1,0:T(8,128)(2,1)S(1)}, bf16[240,128]{1,0:T(8,128)(2,1)S(1)}, u32[]{:S(2)}, u32[]{:S(2)}) collective-permute-start(bf16[240,128]{1,0:T(8,128)(2,1)S(1)} %get-tuple-element.57.mine_ref), channel_id=1, source_target_pairs={{0,16},{2,18},{4,20},{6,22},{8,24},{10,26},{12,28},{14,30},{16,0},... | collective-permute-start | bytes 184328 | tf_op jit(solution)/shard_map/ppermute | solution.py:662
  60.3 1.9 %collective-permute-start.5 = (bf16[8,240,128]{2,1,0:T(8,128)(2,1)S(1)}, bf16[8,240,128]{2,1,0:T(8,128)(2,1)S(1)}, u32[]{:S(2)}, u32[]{:S(2)}) collective-permute-start(bf16[8,240,128]{2,1,0:T(8,128)(2,1)S(1)} %all_to_all.11.mine_ref), channel_id=1, source_target_pairs={{0,1},{1,0},{2,3},{3,2},{4,5},{5,4},{6,7},{7,6},{8,9},{9,8},{10,11... | collective-permute-start | bytes 1474568 | tf_op jit(solution)/shard_map/ppermute | solution.py:683

commit v5 on v3

--- a/solution.py
+++ b/solution.py
@@ -121,7 +121,7 @@
                 pieces.append(jnp.concatenate([tiles[4 * group + q] for group in range(4)], axis=1))
         lhs_scr[pair * 80 : (pair + 1) * 80, :] = jnp.concatenate(pieces, axis=0).astype(BF16)
     total_rows = len(planes) * 40
-    chunk = 160
+    chunk = total_rows
     for part in range(total_rows // chunk):
         product = dot(lhs_scr[part * chunk : (part + 1) * chunk, :], split_ref[...])
         for q in range(5):

time: 64 us -> 64.1 us (level)
  no operation moved by 1% of the time
where the time goes in v5:
time: 64.1 us; the launch traced here: 63.7 us
  blocking collectives  23.2 us (36%)
  Pallas kernels  14.4 us (22%)
  starting transfers between devices  13.1 us (20%)
  waiting for transfers between devices  6.15 us (10%)
  local copies, waits for them, and re-layouts  6.05 us (9%)
  between operations  0.77 us (1%)
    all_to_all x2, blocking collectives, exchange(): lax.all_to_all(parts, 'space', split_axis=0, concat_axis=0, axis_index_gr...  23.2 us
    ppermute x2, starting transfers between devices, from_partner(): lax.ppermute(block, 'space', [(i, i ^ stride) for i in range(lax.axis_siz...  6.9 us
    ppermute x2, starting transfers between devices, passed_along(): return lax.ppermute(block, axis, route)  6.16 us
    ppermute x2, waiting for transfers between devices, from_partner(): lax.ppermute(block, 'space', [(i, i ^ stride) for i in range(lax.axis_siz...  5.71 us
    unnamed x20, local copies, waits for them, and re-layouts  5.02 us
    pallas_call x1, Pallas kernels, local(): call(own_kernel, (like((tall, cells), F32), like((tall, cells), F32), lik...  2.93 us
    pallas_call x1, Pallas kernels, local(): call(functools.partial(forward_kernel, 1.0 / math.sqrt(total_two)), (like...  2.93 us
    pallas_call x1, Pallas kernels, local(): call(functools.partial(sums_kernel, places, rows_two), (like((half, LANES...  2.15 us
  transfers between devices with their start and end apart: 6, of which 3 were waited for; matrix products, arithmetic and copies ran while one was open for 0% of the time, Pallas kernels for 15%

profile of v5, /device:TPU:0, one launch (start us, length us, event | category | flops | bytes accessed | tf_op | source)
XLA Modules:
  0.0 63.7 jit_solution(4491825618849949137)
XLA Ops:
  0.6 1.0 %slice.8 = bf16[4,3,128,128]{3,2,1,0:T(8,128)(2,1)S(1)} slice(bf16[4,4,128,128]{3,2,1,0:T(8,128)(2,1)} %bitcast.9), slice={[0:4], [1:4], [0:128], [0:128]} | slice | bytes 786432 | tf_op jit(solution)/shard_map/slice | solution.py:708
  1.7 4.9 %collective-permute-start = (bf16[4,3,128,128]{3,2,1,0:T(8,128)(2,1)S(1)}, bf16[4,3,128,128]{3,2,1,0:T(8,128)(2,1)S(1)}, u32[]{:S(2)}, u32[]{:S(2)}) collective-permute-start(bf16[4,3,128,128]{3,2,1,0:T(8,128)(2,1)S(1)} %slice.8), channel_id=1, source_target_pairs={{0,2},{2,4},{4,6},{6,8},{8,10},{10,12},{12,14},{14,16},{16,18},{18... | collective-permute-start | bytes 1179656 | tf_op jit(solution)/shard_map/ppermute | solution.py:672
  6.5 0.0 copy-start.2
  6.6 0.9 %copy-done.2 = bf16[864,64]{0,1:T(8,128)(2,1)S(1)} copy-done((bf16[864,64]{0,1:T(8,128)(2,1)S(1)}, bf16[864,64]{0,1:T(8,128)(2,1)}, u32[]{:S(2)}) %copy-start.2) | copy-done | bytes 110616
  7.4 0.7 %copy-done.4 = bf16[108,32]{0,1:T(8,128)(2,1)S(1)} copy-done((bf16[108,32]{0,1:T(8,128)(2,1)S(1)}, bf16[108,32]{0,1:T(8,128)(2,1)}, u32[]{:S(2)}) %copy-start.4) | copy-done | bytes 6936
  8.1 1.2 %copy-done.5 = bf16[8,112,400]{2,1,0:T(8,128)(2,1)S(1)} copy-done((bf16[8,112,400]{2,1,0:T(8,128)(2,1)S(1)}, bf16[8,112,400]{2,1,0:T(8,128)(2,1)}, u32[]{:S(2)}) %copy-start.5) | copy-done | bytes 716824
  9.3 1.1 %copy-done.7 = bf16[8,112,304]{2,1,0:T(8,128)(2,1)S(1)} copy-done((bf16[8,112,304]{2,1,0:T(8,128)(2,1)S(1)}, bf16[8,112,304]{2,1,0:T(8,128)(2,1)}, u32[]{:S(2)}) %copy-start.7) | copy-done | bytes 544792
  10.4 0.4 shard_map.126
  10.8 0.7 %copy-done = bf16[4,1,4,128,128]{4,3,2,1,0:T(8,128)(2,1)S(1)} copy-done((bf16[4,1,4,128,128]{4,3,2,1,0:T(8,128)(2,1)S(1)}, bf16[4,1,4,128,128]{4,3,2,1,0:T(8,128)(2,1)}, u32[]{:S(2)}) %copy-start) | copy-done | bytes 524312
  11.5 0.3 copy-done.6
  11.8 0.2 copy-done.8
  11.9 2.9 %shard_map.127 = (f32[128,1024]{1,0:T(8,128)S(1)}, f32[128,1024]{1,0:T(8,128)S(1)}, f32[128,1024]{1,0:T(8,128)S(1)}, bf16[8,112,1024]{2,1,0:T(8,128)(2,1)S(1)}, f32[112,112]{1,0:T(8,128)S(1)}) custom-call(bf16[4,4,128,128]{3,2,1,0:T(8,128)(2,1)S(1)} %bitcast.10, bf16[256,400]{1,0:T(8,128)(2,1)S(1)} %get-tuple-element.41.wide_ref, ...), custom_call_target="tpu_custom_call" | custom-call | flops 6600000000 | bytes 1048576 | tf_op jit(solution)/shard_map/pallas_call | solution.py:718
  14.9 0.0 collective-permute-done.halo_ref
  14.9 2.9 %shard_map.128 = (bf16[64,1024]{1,0:T(8,128)(2,1)S(1)}, bf16[896,1024]{1,0:T(8,128)(2,1)S(1)}, f32[128,1024]{1,0:T(8,128)S(1)}, bf16[4,112,1024]{2,1,0:T(8,128)(...) custom-call(bf16[4,3,128,128]{3,2,1,0:T(8,128)(2,1)S(1)} %collective-permute-done.halo_ref, ...), custom_call_target="tpu_custom_call" | custom-call | flops 5500000256 | bytes 1048576 | tf_op jit(solution)/shard_map/pallas_call | solution.py:735
  17.9 1.3 %collective-permute-start.3 = (bf16[64,1024]{1,0:T(8,128)(2,1)S(1)}, bf16[64,1024]{1,0:T(8,128)(2,1)S(1)}, u32[]{:S(2)}, u32[]{:S(2)}) collective-permute-start(bf16[64,1024]{1,0:T(8,128)(2,1)S(1)} %get-tuple-element.46.grad_ref), channel_id=1, source_target_pairs={{2,0},{4,2},{6,4},{8,6},{10,8},{12,10},{14,12},{16,14},{18,16},{20... | collective-permute-start | bytes 393224 | tf_op jit(solution)/shard_map/ppermute | solution.py:672
  19.2 6.5 %collective-permute-start.2 = (bf16[8,32,128]{2,1,0:T(8,128)(2,1)S(1)}, bf16[8,32,128]{2,1,0:T(8,128)(2,1)S(1)}, u32[]{:S(2)}, u32[]{:S(2)}) collective-permute-start(bf16[8,32,128]{2,1,0:T(8,128)(2,1)S(1)} %get-tuple-element.50), channel_id=1, source_target_pairs={{0,16},{2,18},{4,20},{6,22},{8,24},{10,26},{12,28},{14,30},{16,0},... | collective-permute-start | bytes 196616 | tf_op jit(solution)/shard_map/ppermute | solution.py:655
  25.7 2.2 %shard_map.129 = (bf16[1792,128]{1,0:T(8,128)(2,1)S(1)}, bf16[1792,128]{1,0:T(8,128)(2,1)S(1)}, f32[8,128]{1,0:T(8,128)S(1)}) custom-call(bf16[896,1024]{1,0:T(8,128)(2,1)S(1)} %get-tuple-element.45.p2_ref, bf16[64,1024]{1,0:T(8,128)(2,1)S(1)} %get-tuple-element.46.grad_ref), custom_call_target="tpu_custom_call" | custom-call | flops 110000000 | bytes 1048576 | tf_op jit(solution)/shard_map/pallas_call | solution.py:756
  27.9 0.1 collective-permute-start.1
  27.9 1.0 %shard_map.130 = (f32[112,112]{1,0:T(8,128)S(1)}, f32[32,144]{1,0:T(8,128)S(1)}, f32[128,1024]{1,0:T(8,128)S(1)}) custom-call(bf16[64,1024]{1,0:T(8,128)(2,1)S(1)} %get-tuple-element.46.grad_ref, bf16[256,512]{1,0:T(8,128)(2,1)S(1)} %get-tuple-element.52.back_ref, f32[128,1024]{1,0:T(8,128)S(1)} %get-tuple-element.53.slope_ref, ...), custom_call_target="tpu_custom_call" | custom-call | flops 110000000 | bytes 1048576 | tf_op jit(solution)/shard_map/pallas_call | solution.py:763
  28.9 1.8 %collective-permute-done.2.refs_1_ = bf16[8,32,128]{2,1,0:T(8,128)(2,1)S(1)} collective-permute-done((bf16[8,32,128]{2,1,0:T(8,128)(2,1)S(1)}, bf16[8,32,128]{2,1,0:T(8,128)(2,1)S(1)}, u32[]{:S(2)}, u32[]{:S(2)}) %collective-permute-start.2) | collective-permute-done | bytes 65568 | tf_op jit(solution)/shard_map/ppermute | solution.py:655
  30.8 0.0 collective-permute-done.3.above_ref
  30.8 0.7 %shard_map.131.small_ref = bf16[128,128]{1,0:T(8,128)(2,1)S(1)} custom-call(bf16[64,1024]{1,0:T(8,128)(2,1)S(1)} %collective-permute-done.3.above_ref, bf16[256,512]{1,0:T(8,128)(2,1)S(1)} %get-tuple-element.52.back_ref, f32[128,1024]{1,0:T(8,128)S(1)} %get-tuple-element.57.high_ref, f32[128,1024]{1,0:T(8,128)S(1)} %get-tuple-element.58.slope_ref, ...), custom_call_target="tpu_custom_call" | custom-call | flops 13200000000 | bytes 1048576 | tf_op jit(solution)/shard_map/pallas_call | solution.py:769
  31.5 0.1 shard_map.132
  31.6 13.0 %all_to_all.10.came_ref = bf16[8,304,128]{2,1,0:T(8,128)(2,1)S(1)} all-to-all(bf16[8,304,128]{2,1,0:T(8,128)(2,1)S(1)} %shard_map.132), channel_id=1, replica_groups={{0,2,6,4,12,14,10,8},{16,18,22,20,28,30,26,24},{1,3,7,5,13,15,11,9},{17..., dimensions={0} | all-to-all | bytes 1245184 | tf_op jit(solution)/shard_map/all_to_all | solution.py:651
  44.6 0.1 shard_map.133
  44.7 0.4 collective-permute-start.4
  45.0 1.0 %shard_map.134 = bf16[64,16,64]{2,1,0:T(8,128)(2,1)} custom-call(bf16[8,64,128]{2,1,0:T(8,128)(2,1)S(1)} %get-tuple-element.64.feat_ref), custom_call_target="tpu_custom_call" | custom-call | flops 1100000000 | bytes 1048576 | tf_op jit(solution)/shard_map/pallas_call | solution.py:783
  46.0 3.9 %collective-permute-done.4.came_ref = bf16[240,128]{1,0:T(8,128)(2,1)S(1)} collective-permute-done((bf16[240,128]{1,0:T(8,128)(2,1)S(1)}, bf16[240,128]{1,0:T(8,128)(2,1)S(1)}, u32[]{:S(2)}, u32[]{:S(2)}) %collective-permute-start.4) | collective-permute-done | bytes 61472 | tf_op jit(solution)/shard_map/ppermute | solution.py:655
  49.9 10.3 %all_to_all.11.mine_ref = bf16[8,240,128]{2,1,0:T(8,128)(2,1)S(1)} all-to-all(bf16[8,240,128]{2,1,0:T(8,128)(2,1)S(1)} %shard_map.135), channel_id=1, replica_groups={{0,2,6,4,12,14,10,8},{16,18,22,20,28,30,26,24},{1,3,7,5,13,15,11,9},{17..., dimensions={0} | all-to-all | bytes 983040 | tf_op jit(solution)/shard_map/all_to_all | solution.py:651
  60.2 1.4 %shard_map.136.begun_ref = f32[864,864]{1,0:T(8,128)} custom-call(bf16[8,240,128]{2,1,0:T(8,128)(2,1)S(1)} %all_to_all.11.mine_ref), custom_call_target="tpu_custom_call" | custom-call | flops 2200000000 | bytes 1048576 | tf_op jit(solution)/shard_map/pallas_call | solution.py:795
  61.6 0.4 collective-permute-done.5.came_ref
  62.0 1.7 %shard_map.137 = (f32[108,108]{1,0:T(8,128)}, f32[864,864]{1,0:T(8,128)}, f32[32,32]{1,0:T(8,128)}, f32[64,64]{1,0:T(8,128)}, f32[32,108]{1,0:T(8,128)}, /*index=5*/f32[64,864]{1,0:T(8,128)}) custom-call(f32[864,864]{1,0:T(8,128)} %shard_map.136.begun_ref, bf16[8,240,128]{2,1,0:T(8,128)(2,1)S(1)} %all_to_all.11.mine_ref, ...), custom_call_target="tpu_custom_call", output_to_operand_aliasing={{1}: (0, {})} | custom-call | flops 2200000000 | bytes 1048576 | tf_op jit(solution)/shard_map/pallas_call | solution.py:817
  (15 shorter events, 0.1 us)
Async XLA Ops:
  1.7 13.2 %collective-permute-start = (bf16[4,3,128,128]{3,2,1,0:T(8,128)(2,1)S(1)}, bf16[4,3,128,128]{3,2,1,0:T(8,128)(2,1)S(1)}, u32[]{:S(2)}, u32[]{:S(2)}) collective-permute-start(bf16[4,3,128,128]{3,2,1,0:T(8,128)(2,1)S(1)} %slice.8), channel_id=1, source_target_pairs={{0,2},{2,4},{4,6},{6,8},{8,10},{10,12},{12,14},{14,16},{16,18},{18... | collective-permute-start | bytes 1179656 | tf_op jit(solution)/shard_map/ppermute | solution.py:672
  6.5 0.9 %copy-start.2 = (bf16[864,64]{0,1:T(8,128)(2,1)S(1)}, bf16[864,64]{0,1:T(8,128)(2,1)}, u32[]{:S(2)}) copy-start(bf16[864,64]{0,1:T(8,128)(2,1)} %param.9) | copy-start | bytes 331780
  7.4 0.7 %copy-start.4 = (bf16[108,32]{0,1:T(8,128)(2,1)S(1)}, bf16[108,32]{0,1:T(8,128)(2,1)}, u32[]{:S(2)}) copy-start(bf16[108,32]{0,1:T(8,128)(2,1)} %param.8) | copy-start | bytes 20740
  8.1 1.2 %copy-start.5 = (bf16[8,112,400]{2,1,0:T(8,128)(2,1)S(1)}, bf16[8,112,400]{2,1,0:T(8,128)(2,1)}, u32[]{:S(2)}) copy-start(bf16[8,112,400]{2,1,0:T(8,128)(2,1)} %constant.7.clone.own_rows_ref.rows_ref) | copy-start | bytes 2150404
  9.3 1.1 %copy-start.7 = (bf16[8,112,304]{2,1,0:T(8,128)(2,1)S(1)}, bf16[8,112,304]{2,1,0:T(8,128)(2,1)}, u32[]{:S(2)}) copy-start(bf16[8,112,304]{2,1,0:T(8,128)(2,1)} %constant.6.clone.halo_rows_ref) | copy-start | bytes 1634308
  10.4 1.0 %copy-start = (bf16[4,1,4,128,128]{4,3,2,1,0:T(8,128)(2,1)S(1)}, bf16[4,1,4,128,128]{4,3,2,1,0:T(8,128)(2,1)}, u32[]{:S(2)}) copy-start(bf16[4,1,4,128,128]{4,3,2,1,0:T(8,128)(2,1)} %param.7) | copy-start | bytes 1572868
  10.4 1.3 %copy-start.6 = (bf16[8,112,400]{2,1,0:T(8,128)(2,1)S(1)}, bf16[8,112,400]{2,1,0:T(8,128)(2,1)}, u32[]{:S(2)}) copy-start(bf16[8,112,400]{2,1,0:T(8,128)(2,1)} %constant.7.clone.own_rows_ref.rows_ref) | copy-start | bytes 2150404
  10.4 1.5 %copy-start.8 = (bf16[512,640]{1,0:T(8,128)(2,1)S(1)}, bf16[512,640]{1,0:T(8,128)(2,1)}, u32[]{:S(2)}) copy-start(bf16[512,640]{1,0:T(8,128)(2,1)} %constant.8.clone.split_ref) | copy-start | bytes 1966084
  11.9 3.0 %copy-start.1 = (bf16[64,1,1,1024]{3,0,2,1:T(8,128)(2,1)S(1)}, bf16[64,1,1,1024]{3,0,2,1:T(8,128)(2,1)}, u32[]{:S(2)}) copy-start(bf16[64,1,1,1024]{3,0,2,1:T(8,128)(2,1)} %param.10) | copy-start | bytes 393220
  11.9 3.0 %copy-start.3 = (bf16[864,64]{0,1:T(8,128)(2,1)S(1)}, bf16[864,64]{0,1:T(8,128)(2,1)}, u32[]{:S(2)}) copy-start(bf16[864,64]{0,1:T(8,128)(2,1)} %param.9) | copy-start | bytes 331780
  11.9 3.0 %copy-start.9 = (bf16[4,112,304]{2,1,0:T(8,128)(2,1)S(1)}, bf16[4,112,304]{2,1,0:T(8,128)(2,1)}, u32[]{:S(2)}) copy-start(bf16[4,112,304]{2,1,0:T(8,128)(2,1)} %constant.11.rows_ref) | copy-start | bytes 817156
  17.9 12.9 %collective-permute-start.3 = (bf16[64,1024]{1,0:T(8,128)(2,1)S(1)}, bf16[64,1024]{1,0:T(8,128)(2,1)S(1)}, u32[]{:S(2)}, u32[]{:S(2)}) collective-permute-start(bf16[64,1024]{1,0:T(8,128)(2,1)S(1)} %get-tuple-element.46.grad_ref), channel_id=1, source_target_pairs={{2,0},{4,2},{6,4},{8,6},{10,8},{12,10},{14,12},{16,14},{18,16},{20... | collective-permute-start | bytes 393224 | tf_op jit(solution)/shard_map/ppermute | solution.py:672
  19.2 11.6 %collective-permute-start.2 = (bf16[8,32,128]{2,1,0:T(8,128)(2,1)S(1)}, bf16[8,32,128]{2,1,0:T(8,128)(2,1)S(1)}, u32[]{:S(2)}, u32[]{:S(2)}) collective-permute-start(bf16[8,32,128]{2,1,0:T(8,128)(2,1)S(1)} %get-tuple-element.50), channel_id=1, source_target_pairs={{0,16},{2,18},{4,20},{6,22},{8,24},{10,26},{12,28},{14,30},{16,0},... | collective-permute-start | bytes 196616 | tf_op jit(solution)/shard_map/ppermute | solution.py:655
  27.9 3.6 %collective-permute-start.1 = (bf16[1792,128]{1,0:T(8,128)(2,1)S(1)}, bf16[1792,128]{1,0:T(8,128)(2,1)S(1)}, u32[]{:S(2)}, u32[]{:S(2)}) collective-permute-start(bf16[1792,128]{1,0:T(8,128)(2,1)S(1)} %get-tuple-element.48), channel_id=1, source_target_pairs={{0,1},{1,0},{2,3},{3,2},{4,5},{5,4},{6,7},{7,6},{8,9},{9,8},{10,11... | collective-permute-start | bytes 1376264 | tf_op jit(solution)/shard_map/ppermute | solution.py:676
  44.7 5.2 %collective-permute-start.4 = (bf16[240,128]{1,0:T(8,128)(2,1)S(1)}, bf16[240,128]{1,0:T(8,128)(2,1)S(1)}, u32[]{:S(2)}, u32[]{:S(2)}) collective-permute-start(bf16[240,128]{1,0:T(8,128)(2,1)S(1)} %get-tuple-element.63.mine_ref), channel_id=1, source_target_pairs={{0,16},{2,18},{4,20},{6,22},{8,24},{10,26},{12,28},{14,30},{16,0},... | collective-permute-start | bytes 184328 | tf_op jit(solution)/shard_map/ppermute | solution.py:655
  60.2 1.9 %collective-permute-start.5 = (bf16[8,240,128]{2,1,0:T(8,128)(2,1)S(1)}, bf16[8,240,128]{2,1,0:T(8,128)(2,1)S(1)}, u32[]{:S(2)}, u32[]{:S(2)}) collective-permute-start(bf16[8,240,128]{2,1,0:T(8,128)(2,1)S(1)} %all_to_all.11.mine_ref), channel_id=1, source_target_pairs={{0,1},{1,0},{2,3},{3,2},{4,5},{5,4},{6,7},{7,6},{8,9},{9,8},{10,11... | collective-permute-start | bytes 1474568 | tf_op jit(solution)/shard_map/ppermute | solution.py:676
